TPU v7x, 32 devices: a whole 2x2x4 slice. The times are simulated.
32 devices in a mesh: group: 4 (over y, x), rep: 8 (over z, core).
Axes of the slice: x: 2, y: 2, z: 4, core: 2. Of those that a mesh axis runs over, the one named last changes fastest.
Arguments:
- hidden_in: bfloat16 [32, 1024, 768], P(('group', 'rep')), may hold values from -6 to 6
- out_grad: bfloat16 [32, 1024, 768], P(('group', 'rep')), may hold values from -6 to 6
- segment_ids: int32 [32, 1024], P(('group', 'rep')), may hold values from 0 to 3, never falling along the last dimension, each value on 1 to 800 neighbouring positions
- rand_blocks: int32 [32, 16, 3], P(('group', 'rep')), may hold values from 0 to 15
- w_qkv: float32 [768, 2304], P('group'), may hold values from -0.21875 to 0.21875
- w_out: float32 [768, 768], P('group'), may hold values from -0.875 to 0.875
- w_in: float32 [768, 3072], P('group'), may hold values from -0.21875 to 0.21875
- w_down: float32 [3072, 768], P('group'), may hold values from -0.109375 to 0.109375
- vec_params: float32 [768, 8], P('group'), may hold values from -0.6 to 1.6, as said below
- bias_hidden: float32 [3072], P('group'), may hold values from -1.5 to 1.5
- moments_qkv: float32 [2, 768, 2304], P(None, 'group'), may hold values from -4 to 4, as said below
- moments_out: float32 [2, 768, 768], P(None, 'group'), may hold values from -4 to 4, as said below
- moments_in: float32 [2, 768, 3072], P(None, 'group'), may hold values from -4 to 4, as said below
- moments_down: float32 [2, 3072, 768], P(None, 'group'), may hold values from -4 to 4, as said below
- moments_vec: float32 [2, 768, 8], P(None, 'group'), may hold values from -4 to 4, as said below
- moments_bias: float32 [2, 3072], P(None, 'group'), may hold values from -4 to 4, as said below
Outputs:
- layer_out: float32 [32, 1024, 768], P(('group', 'rep'))
- grad_in: float32 [32, 1024, 768], P(('group', 'rep'))
- grad_w_qkv: float32 [768, 2304], P('group')
- grad_w_out: float32 [768, 768], P('group')
- grad_w_in: float32 [768, 3072], P('group')
- grad_w_down: float32 [3072, 768], P('group')
- grad_vec: float32 [768, 8], P('group')
- grad_bias: float32 [3072], P('group')
- new_w_qkv: float32 [768, 2304], P('group')
- new_w_out: float32 [768, 768], P('group')
- new_w_in: float32 [768, 3072], P('group')
- new_w_down: float32 [3072, 768], P('group')
- new_vec: float32 [768, 8], P('group')
- new_bias: float32 [3072], P('group')
- new_mom_qkv: float32 [2, 768, 2304], P(None, 'group')
- new_mom_out: float32 [2, 768, 768], P(None, 'group')
- new_mom_in: float32 [2, 768, 3072], P(None, 'group')
- new_mom_down: float32 [2, 3072, 768], P(None, 'group')
- new_mom_vec: float32 [2, 768, 8], P(None, 'group')
- new_mom_bias: float32 [2, 3072], P(None, 'group')
Inputs may be any that keep to these rules, and one draw needn't show every extreme that they name: `moments_qkv`: index 0 along the first dimension holds first moments, index 1 second moments, which are 0.5 or more. `moments_out`: like moments_qkv. `moments_in`: like moments_qkv. `moments_down`: like moments_qkv. `moments_vec`: like moments_qkv. `moments_bias`: like moments_qkv. `vec_params`: the two gain columns 3 and 6 lie in 0.4 to 1.6, the others in -0.6 to 0.6.
All inputs are finite; a program needn't handle non-finite values.
Results may differ from a plain program's by a relative error of at most 0.017.
The roundings to bfloat16 on the way count: a program that leaves them out, or rounds other values in their place, can miss the bound.
Values may be sent and summed in bfloat16 or wider, within the bound.
No kernel may reach another device: no remote copies, remote signals or barrier semaphores. Data moves between devices by JAX's collectives and lax.ppermute only.
A program may use at most 320 MiB of HBM per device.

v0:
```python
import jax
import jax.numpy as jnp
from jax import lax
from jax.sharding import PartitionSpec as P

HEAD_DIM = 64
STEP = 4


norm_eps = 1e-05
adam_eps = 1e-08
matrix_decay = 0.1
step_rate = 0.1
masked_score = -1e30


def attend_mask(segments, randoms):
    blocks = randoms.shape[0]
    block_len = segments.shape[0] // blocks
    block_ids = jnp.arange(blocks)
    nearby = jnp.abs(block_ids[:, None] - block_ids[None, :]) <= 1
    edge_row = (block_ids == 0) | (block_ids == blocks - 1)
    picked = jnp.any(randoms[:, :, None] == block_ids[None, None, :], axis=1)
    allowed = nearby | edge_row[:, None] | edge_row[None, :] | picked
    tokens = jnp.repeat(jnp.repeat(allowed, block_len, axis=0), block_len, axis=1)
    return tokens & (segments[:, None] == segments[None, :])


def layer_norm(residual, gain_vec, shift_vec):
    center = residual - jnp.mean(residual, axis=-1, keepdims=True)
    spread = jnp.mean(center * center, axis=-1, keepdims=True)
    inverse = lax.rsqrt(spread + norm_eps)
    normed = center * inverse
    return (normed * gain_vec + shift_vec, normed, inverse)


def norm_back(grad_out, gain_vec, normed, inverse):
    grad_normed = grad_out * gain_vec
    mean_plain = jnp.mean(grad_normed, axis=-1, keepdims=True)
    mean_mixed = jnp.mean(grad_normed * normed, axis=-1, keepdims=True)
    return inverse * (grad_normed - mean_plain - normed * mean_mixed)


def gelu_exact(value_vectors):
    return jax.nn.gelu(value_vectors, approximate=False)


def masked_scores(query_vectors, key_matrix_rows, allowed):
    raw = jnp.einsum(
        "ntb,otb->tno", query_vectors, key_matrix_rows, preferred_element_type=jnp.float32
    ) * query_vectors.shape[-1] ** (-0.5)
    return jnp.where(allowed[None], raw, masked_score)


def attend_forward(packed):
    query_vectors, key_matrix_rows, value_vectors, allowed = packed
    scores = masked_scores(query_vectors, key_matrix_rows, allowed)
    top_score = jnp.max(scores, axis=-1, keepdims=True)
    exponent = jnp.exp(scores - top_score)
    partition = jnp.sum(exponent, axis=-1, keepdims=True)
    attention_weights_soft = (exponent / partition).astype(jnp.bfloat16)
    attended = jnp.einsum(
        "tys,stv->ytv", attention_weights_soft, value_vectors, preferred_element_type=jnp.float32
    ).astype(jnp.bfloat16)
    return (attended, (top_score + jnp.log(partition))[..., 0])


def attend_backward(packed):
    query_vectors, key_matrix_rows, value_vectors, allowed, log_total, attention_output_gradient = (
        packed
    )
    scores = masked_scores(query_vectors, key_matrix_rows, allowed)
    attention_weights_soft = jnp.exp(scores - log_total[..., None])
    probability_gradient = jnp.einsum(
        "ntb,otb->tno", attention_output_gradient, value_vectors, preferred_element_type=jnp.float32
    )
    grad_val = jnp.einsum(
        "saw,aso->wso",
        attention_weights_soft.astype(jnp.bfloat16),
        attention_output_gradient,
        preferred_element_type=jnp.float32,
    )
    inner_sum = jnp.sum(attention_weights_soft * probability_gradient, axis=-1, keepdims=True)
    logit_gradient = (attention_weights_soft * (probability_gradient - inner_sum)).astype(
        jnp.bfloat16
    )
    logit_scale = query_vectors.shape[-1] ** (-0.5)
    grad_query = (
        jnp.einsum(
            "tys,stv->ytv", logit_gradient, key_matrix_rows, preferred_element_type=jnp.float32
        )
        * logit_scale
    ).astype(jnp.bfloat16)
    grad_key = (
        jnp.einsum(
            "saw,aso->wso", logit_gradient, query_vectors, preferred_element_type=jnp.float32
        )
        * logit_scale
    ).astype(jnp.bfloat16)
    return (grad_query, grad_key, grad_val.astype(jnp.bfloat16))


def adam_step(weight, moment, gradient, decay, correct, rate):
    first_m = 0.5 * moment[0] + 0.5 * gradient
    second_m = 0.5 * moment[1] + 0.5 * gradient * gradient
    update = first_m / correct / (jnp.sqrt(second_m / correct) + adam_eps) + decay * weight
    return (weight - rate * update, jnp.stack([first_m, second_m]))


def local(
    hidden_in,
    out_grad,
    segment_ids,
    rand_blocks,
    w_qkv,
    w_out,
    w_in,
    w_down,
    vec_params,
    bias_hidden,
    moments_qkv,
    moments_out,
    moments_in,
    moments_down,
    moments_vec,
    moments_bias,
):
    full_qkv, full_out, full_in, full_down, full_vec, full_bias = (
        lax.all_gather(w_qkv.astype(jnp.bfloat16), "group", axis=0, tiled=True),
        lax.all_gather(w_out.astype(jnp.bfloat16), "group", axis=0, tiled=True),
        lax.all_gather(w_in.astype(jnp.bfloat16), "group", axis=0, tiled=True),
        lax.all_gather(w_down.astype(jnp.bfloat16), "group", axis=0, tiled=True),
        lax.all_gather(vec_params.astype(jnp.bfloat16), "group", axis=0, tiled=True),
        lax.all_gather(bias_hidden.astype(jnp.bfloat16), "group", axis=0, tiled=True),
    )
    vectors = full_vec.astype(jnp.float32)
    bias_q, bias_v, bias_o, gain_one, shift_one, bias_d, gain_two, shift_two = [
        vectors[:, column] for column in range(8)
    ]
    bias_full = full_bias.astype(jnp.float32)
    seq_count, seq_len, feat_width = hidden_in.shape
    row_count = seq_count * seq_len
    head_count = feat_width // HEAD_DIM
    split = (seq_count, seq_len, head_count, HEAD_DIM)
    x_rows = hidden_in.reshape(row_count, feat_width)
    qkv_rows = jnp.dot(x_rows, full_qkv, preferred_element_type=jnp.float32)
    query_rows = (qkv_rows[:, :feat_width] + bias_q).astype(jnp.bfloat16).reshape(split)
    key_matrix_rows = qkv_rows[:, feat_width : 2 * feat_width].astype(jnp.bfloat16).reshape(split)
    value_rows = (qkv_rows[:, 2 * feat_width :] + bias_v).astype(jnp.bfloat16).reshape(split)
    allowed = jax.vmap(attend_mask)(segment_ids, rand_blocks)
    attended, log_total = lax.map(
        attend_forward, (query_rows, key_matrix_rows, value_rows, allowed)
    )
    att_rows = attended.reshape(row_count, feat_width)
    residual_one = x_rows.astype(jnp.float32) + (
        jnp.dot(att_rows, full_out, preferred_element_type=jnp.float32) + bias_o
    )
    norm_one, normed_one, inverse_one = layer_norm(residual_one, gain_one, shift_one)
    first_low = norm_one.astype(jnp.bfloat16)
    hidden = jnp.dot(first_low, full_in, preferred_element_type=jnp.float32) + bias_full
    active, gelu_pull = jax.vjp(gelu_exact, hidden)
    active_low = active.astype(jnp.bfloat16)
    residual_two = norm_one + (
        jnp.dot(active_low, full_down, preferred_element_type=jnp.float32) + bias_d
    )
    result, normed_two, inverse_two = layer_norm(residual_two, gain_two, shift_two)
    layer_out = result.reshape(hidden_in.shape)
    grad_y = out_grad.reshape(row_count, feat_width).astype(jnp.float32)
    grad_gain_two = jnp.sum(grad_y * normed_two, axis=0)
    grad_shift_two = jnp.sum(grad_y, axis=0)
    grad_res_two = norm_back(grad_y, gain_two, normed_two, inverse_two)
    grad_down_low = grad_res_two.astype(jnp.bfloat16)
    grad_bias_d = jnp.sum(grad_res_two, axis=0)
    grad_w_down = jnp.einsum(
        "rf,rd->fd", active_low, grad_down_low, preferred_element_type=jnp.float32
    )
    grad_active = jnp.einsum(
        "rd,fd->rf", grad_down_low, full_down, preferred_element_type=jnp.float32
    )
    grad_hidden = gelu_pull(grad_active)[0].astype(jnp.bfloat16)
    grad_bias_hidden = jnp.sum(grad_hidden.astype(jnp.float32), axis=0)
    grad_w_in = jnp.einsum("rd,rf->df", first_low, grad_hidden, preferred_element_type=jnp.float32)
    grad_first = grad_res_two + jnp.einsum(
        "rf,df->rd", grad_hidden, full_in, preferred_element_type=jnp.float32
    )
    grad_gain_one = jnp.sum(grad_first * normed_one, axis=0)
    grad_shift_one = jnp.sum(grad_first, axis=0)
    grad_res_one = norm_back(grad_first, gain_one, normed_one, inverse_one)
    grad_bias_o = jnp.sum(grad_res_one, axis=0)
    grad_branch_low = grad_res_one.astype(jnp.bfloat16)
    grad_w_out = jnp.einsum(
        "rd,re->de", att_rows, grad_branch_low, preferred_element_type=jnp.float32
    )
    attention_output_gradient = jnp.einsum(
        "re,de->rd", grad_branch_low, full_out, preferred_element_type=jnp.float32
    ).astype(jnp.bfloat16)
    grad_query, grad_key, grad_value = lax.map(
        attend_backward,
        (
            query_rows,
            key_matrix_rows,
            value_rows,
            allowed,
            log_total,
            attention_output_gradient.reshape(split),
        ),
    )
    query_grad_rows = grad_query.reshape(row_count, feat_width)
    value_grad_rows = grad_value.reshape(row_count, feat_width)
    grad_qkv = jnp.concatenate(
        [query_grad_rows, grad_key.reshape(row_count, feat_width), value_grad_rows], axis=1
    )
    grad_bias_q = jnp.sum(query_grad_rows.astype(jnp.float32), axis=0)
    grad_bias_v = jnp.sum(value_grad_rows.astype(jnp.float32), axis=0)
    grad_w_qkv = jnp.einsum("rd,re->de", x_rows, grad_qkv, preferred_element_type=jnp.float32)
    grad_x = grad_res_one + jnp.einsum(
        "re,de->rd", grad_qkv, full_qkv, preferred_element_type=jnp.float32
    )
    grad_in = grad_x.reshape(hidden_in.shape)
    grad_vec = jnp.stack(
        [
            grad_bias_q,
            grad_bias_v,
            grad_bias_o,
            grad_gain_one,
            grad_shift_one,
            grad_bias_d,
            grad_gain_two,
            grad_shift_two,
        ],
        axis=1,
    )
    inverse_count = 1.0 / (seq_count * lax.axis_size("group") * lax.axis_size("rep"))
    correct = 1.0 - 0.5**STEP
    masters = (w_qkv, w_out, w_in, w_down, vec_params, bias_hidden)
    moments = (moments_qkv, moments_out, moments_in, moments_down, moments_vec, moments_bias)
    decays = (matrix_decay, matrix_decay, matrix_decay, matrix_decay, 0.0, 0.0)
    shard_qkv, shard_out, shard_in, shard_down, shard_vec, shard_bias = (
        lax.psum_scatter(grad_w_qkv, "group", scatter_dimension=0, tiled=True),
        lax.psum_scatter(grad_w_out, "group", scatter_dimension=0, tiled=True),
        lax.psum_scatter(grad_w_in, "group", scatter_dimension=0, tiled=True),
        lax.psum_scatter(grad_w_down, "group", scatter_dimension=0, tiled=True),
        lax.psum_scatter(grad_vec, "group", scatter_dimension=0, tiled=True),
        lax.psum_scatter(grad_bias_hidden, "group", scatter_dimension=0, tiled=True),
    )
    totals = lax.psum((shard_qkv, shard_out, shard_in, shard_down, shard_vec, shard_bias), "rep")
    grads_out = [total * inverse_count for total in totals]
    updated = [
        adam_step(master, moment, gradient, decay, correct, step_rate)
        for master, moment, gradient, decay in zip(masters, moments, grads_out, decays)
    ]
    new_weights = [pair[0] for pair in updated]
    new_moments = [pair[1] for pair in updated]
    return (
        layer_out,
        grad_in,
        grads_out[0],
        grads_out[1],
        grads_out[2],
        grads_out[3],
        grads_out[4],
        grads_out[5],
        new_weights[0],
        new_weights[1],
        new_weights[2],
        new_weights[3],
        new_weights[4],
        new_weights[5],
        new_moments[0],
        new_moments[1],
        new_moments[2],
        new_moments[3],
        new_moments[4],
        new_moments[5],
    )


def solution(mesh):
    return jax.shard_map(
        local,
        mesh=mesh,
        in_specs=(
            P(("group", "rep"), None, None),
            P(("group", "rep"), None, None),
            P(("group", "rep"), None),
            P(("group", "rep"), None, None),
            P("group", None),
            P("group", None),
            P("group", None),
            P("group", None),
            P("group", None),
            P("group"),
            P(None, "group", None),
            P(None, "group", None),
            P(None, "group", None),
            P(None, "group", None),
            P(None, "group", None),
            P(None, "group"),
        ),
        out_specs=(
            P(("group", "rep"), None, None),
            P(("group", "rep"), None, None),
            P("group", None),
            P("group", None),
            P("group", None),
            P("group", None),
            P("group", None),
            P("group"),
            P("group", None),
            P("group", None),
            P("group", None),
            P("group", None),
            P("group", None),
            P("group"),
            P(None, "group", None),
            P(None, "group", None),
            P(None, "group", None),
            P(None, "group", None),
            P(None, "group", None),
            P(None, "group"),
        ),
        check_vma=False,
    )
```

profile of v0, /device:TPU:0, one launch (start us, length us, event | category | flops | bytes accessed | tf_op | source)
XLA Modules:
  0.0 961.2 jit_solution(17610943252683774912)
XLA Ops:
  38.4 22.1 %all-gather.7.cloned.1.call-done = bf16[768,2304]{1,0:T(8,128)(2,1)} async-done(((bf16[192,2304]{1,0:T(8,128)(2,1)}), bf16[768,2304]{1,0:T(8,128)(2,1)}) %all-gather.7.cloned.1.call-update) | async-done | bytes 3538960 | tf_op jit(solution)/shard_map/all_gather | solution.py:129
  77.4 19.5 %fusion.6 = (f32[12,1024]{1,0:T(8,128)S(1)}, f32[12,1024,1024]{1,2,0:T(8,128)}) fusion(pred[1024,1024]{0,1:T(8,128)(4,1)S(1)} %bitcast_and_fusion, bf16[1024,12,64]{0,2,1:T(8,128)(2,1)S(1)} %bitcast.184, bf16[1024,12,64]{0,2,1:T(8,128)(2,1)} %bitcast.190), kind=kOutput, calls=%fused_computation.12 | convolution fusion | flops 1648349184 | bytes 54575104 | tf_op jit(solution)/shard_map/while/body/eval_jaxpr/ntb,otb->tno/dot_general | solution.py:49
  96.9 21.7 %fusion = f32[12,1024]{1,0:T(8,128)S(1)} fusion(f32[12,1024]{1,0:T(8,128)S(1)} %get-tuple-element.204, f32[12,1024,1024]{1,2,0:T(8,128)} %get-tuple-element.205, pred[1024,1024]{0,1:T(8,128)(4,1)S(1)} %bitcast_and_fusion), kind=kLoop, calls=%fused_computation.6 | loop fusion | flops 50319360 | bytes 51478528 | tf_op jit(solution)/shard_map/while/body/eval_jaxpr/reduce_sum | solution.py:60
  119.3 32.8 %fusion.29 = bf16[12,64,1024]{2,1,0:T(8,128)(2,1)} fusion(bf16[1024,12,64]{0,2,1:T(8,128)(2,1)S(1)} %bitcast.192, f32[12,1024]{1,0:T(8,128)S(1)} %fusion, f32[12,1024]{1,0:T(8,128)S(1)} %get-tuple-element.204, f32[12,1024,1024]{1,2,0:T(8,128)} %get-tuple-element.205, pred[1024,1024]{0,1:T(8,128)(4,1)S(1)} %bitcast_and_fusion), kind=kOutput, calls=%fused_computation.83 | convolution fusion | flops 1674313728 | bytes 54624256 | tf_op jit(solution)/shard_map/while/body/eval_jaxpr/tys,stv->ytv/dot_general | solution.py:62
  156.4 38.3 %multiply_convert_fusion.1 = (bf16[1024,3072]{1,0:T(8,128)(2,1)}, f32[1024,3072]{1,0:T(8,128)}, f32[1024,3072]{1,0:T(8,128)}) fusion(f32[3072]{0:T(1024)S(1)} %bitcast.201, bf16[768,3072]{1,0:T(8,128)(2,1)} %all-gather.11.cloned.1.call-done, f32[1024,768]{0,1:T(8,128)S(1)} %get-tuple-element.207, f32[768]{0:T(1024)S(1)} %get-tuple-element.162, ...), kind=kOutput, calls=%fused_computation.16 | convolution fusion | flops 5043388416 | bytes 39348224 | tf_op jit(solution)/shard_map/dot_general | solution.py:160
  194.7 14.9 %all-gather.13.cloned.1.call-done = bf16[3072,768]{1,0:T(8,128)(2,1)} async-done(((bf16[768,768]{1,0:T(8,128)(2,1)}), bf16[3072,768]{1,0:T(8,128)(2,1)}) %all-gather.13.cloned.1.call-update) | async-done | bytes 4718608 | tf_op jit(solution)/shard_map/all_gather | solution.py:132
  209.6 9.8 %fusion.70 = (f32[1024]{0:T(1024)S(1)}, f32[1024,768]{0,1:T(8,128)S(1)}) fusion(f32[768]{0:T(1024)S(1)} %copy-done.48, bf16[1024,3072]{1,0:T(8,128)(2,1)} %get-tuple-element.189, bf16[3072,768]{1,0:T(8,128)(2,1)} %all-gather.13.cloned.1.call-done, f32[768]{0:T(1024)S(1)} %get-tuple-element.162, f32[768]{0:T(1024)S(1)} %get-tuple-element.163, ...), kind=kOutput, calls=%fused_computation.161 | convolution fusion | flops 4837342208 | bytes 17323008 | tf_op jit(solution)/shard_map/dot_general | solution.py:164
  222.8 20.7 %convert_reduce_fusion = (f32[3072]{0:T(1024)}, bf16[1024,3072]{1,0:T(8,128)(2,1)}) fusion(f32[1024,3072]{1,0:T(8,128)} %get-tuple-element.190, bf16[3072,768]{1,0:T(8,128)(2,1)} %all-gather.13.cloned.1.call-done, f32[1024]{0:T(1024)S(1)} %get-tuple-element.220, f32[1024,768]{0,1:T(8,128)S(1)} %get-tuple-element.210, ...), kind=kOutput, calls=%fused_computation.14 | convolution fusion | flops 4892390400 | bytes 40938496 | tf_op jit(solution)/shard_map/rd,fd->rf/dot_general | solution.py:177
  243.6 12.3 %multiply_reduce_fusion.1 = (f32[768]{0:T(1024)}, f32[1024]{0:T(1024)S(1)}, f32[1024]{0:T(1024)S(1)}, f32[768]{0:T(1024)}, f32[1024,768]{0,1:T(8,128)S(1)}) fusion(f32[1024,768]{0,1:T(8,128)} %copy-done.7, f32[1024]{0:T(1024)S(1)} %add_rsqrt_fusion.1, f32[1024]{0:T(1024)S(1)} %broadcast_multiply_fusion.11, f32[768]{0:T(1024)S(1)} %get-tuple-element.163, ...), kind=kOutput, calls=%fused_computation.52 | convolution fusion | flops 4845989888 | bytes 22065152 | tf_op jit(solution)/shard_map/rf,df->rd/dot_general | solution.py:183
  260.4 21.0 %convert_reduce_fusion.2 = (f32[12,64]{1,0:T(8,128)S(1)}, bf16[12,64,1024]{2,1,0:T(8,128)(2,1)}) fusion(bf16[1024,12,64]{0,2,1:T(8,128)(2,1)S(1)} %bitcast.198, f32[12,1024]{1,0:T(8,128)S(1)} %copy-done.33, f32[12,1024,1024]{1,2,0:T(8,128)} %get-tuple-element.205, pred[1024,1024]{0,1:T(8,128)(4,1)S(1)} %copy-done.1), kind=kOutput, calls=%fused_computation.53 | convolution fusion | flops 1663302912 | bytes 54578176 | tf_op jit(solution)/shard_map/while/body/eval_jaxpr/saw,aso->wso/dot_general | solution.py:77
  281.3 35.1 %multiply_reduce_fusion = (f32[12,1024]{1,0:T(8,128)S(1)}, f32[12,1024,1024]{1,2,0:T(8,128)}) fusion(f32[12,1024]{1,0:T(8,128)S(1)} %copy-done.33, f32[12,1024,1024]{1,2,0:T(8,128)} %get-tuple-element.205, pred[1024,1024]{0,1:T(8,128)(4,1)S(1)} %copy-done.1, bf16[1024,12,64]{0,2,1:T(8,128)(2,1)} %bitcast.199, bf16[1024,12,64]{0,2,1:T(8,128)(2,1)S(1)} %bitcast.193), kind=kOutput, calls=%fused_computation.1 | convolution fusion | flops 1673515008 | bytes 104955904 | tf_op jit(solution)/shard_map/while/body/eval_jaxpr/ntb,otb->tno/dot_general | solution.py:74
  316.4 41.1 %multiply_convert_fusion = bf16[12,1024,1024]{1,2,0:T(8,128)(2,1)} fusion(f32[12,1024,1024]{1,2,0:T(8,128)} %get-tuple-element.213, f32[12,1024]{1,0:T(8,128)S(1)} %get-tuple-element.212, f32[12,1024]{1,0:T(8,128)S(1)} %copy-done.33, f32[12,1024,1024]{1,2,0:T(8,128)} %get-tuple-element.205, pred[1024,1024]{0,1:T(8,128)(4,1)S(1)} %copy-done.1), kind=kLoop, calls=%fused_computation | loop fusion | flops 75497472 | bytes 126976000 | tf_op jit(solution)/shard_map/while/body/eval_jaxpr/convert_element_type | solution.py:84
  357.6 13.9 %multiply_convert_fusion.2 = bf16[12,64,1024]{2,1,0:T(8,128)(2,1)} fusion(bf16[1024,12,64]{0,2,1:T(8,128)(2,1)S(1)} %bitcast.185, bf16[12,1024,1024]{1,2,0:T(8,128)(2,1)} %multiply_convert_fusion), kind=kOutput, calls=%fused_computation.56 | convolution fusion | flops 1612185600 | bytes 28311552 | tf_op jit(solution)/shard_map/while/body/eval_jaxpr/saw,aso->wso/dot_general | solution.py:95
  371.5 13.3 %convert_reduce_fusion.3 = (f32[12,64]{1,0:T(8,128)S(1)}, bf16[12,64,1024]{2,1,0:T(8,128)(2,1)S(1)}) fusion(bf16[1024,12,64]{0,2,1:T(8,128)(2,1)} %bitcast.191, bf16[12,1024,1024]{1,2,0:T(8,128)(2,1)} %multiply_convert_fusion), kind=kOutput, calls=%fused_computation.54 | convolution fusion | flops 1613757696 | bytes 28314624 | tf_op jit(solution)/shard_map/while/body/eval_jaxpr/tys,stv->ytv/dot_general | solution.py:89
  408.6 12.0 %fusion.59 = f32[768,3072]{1,0:T(8,128)} fusion(bf16[1024,3072]{1,0:T(8,128)(2,1)} %get-tuple-element.219, f32[1024,768]{0,1:T(8,128)S(1)} %copy-done.9, f32[768]{0:T(1024)S(1)} %copy-done.47, f32[768]{0:T(1024)S(1)} %get-tuple-element.163, f32[1024]{0:T(1024)S(1)} %add_rsqrt_fusion.1, f32[1024]{0:T(1024)S(1)} %broadcast_multiply_fusion.11), kind=kOutput, calls=%fused_computation.155 | convolution fusion | flops 4835770368 | bytes 18888704 | tf_op jit(solution)/shard_map/rd,rf->df/dot_general | solution.py:182
  422.5 10.8 %fusion.36 = f32[3072,768]{1,0:T(8,128)} fusion(bf16[1024,3072]{1,0:T(8,128)(2,1)} %get-tuple-element.189, bf16[1,1024,768]{1,2,0:T(8,128)(2,1)} %copy.115, f32[1024,768]{0,1:T(8,128)S(1)} %copy-done.3, f32[1024]{0:T(1024)S(1)} %get-tuple-element.220, f32[1024]{0:T(1024)S(1)} %get-tuple-element.221, f32[768]{0:T(1024)S(1)} %copy-done.35, ...), kind=kOutput, calls=%fused_computation.94 | convolution fusion | flops 4838916096 | bytes 20466688 | tf_op jit(solution)/shard_map/rf,rd->fd/dot_general | solution.py:174
  440.4 39.7 %reduce-scatter.16.cloned.1.call-done = f32[192,2304]{1,0:T(8,128)} async-done(((f32[768,2304]{1,0:T(8,128)}), f32[192,2304]{1,0:T(8,128)}) %reduce-scatter.16.cloned.1.call-update) | async-done | bytes 1769488
  483.0 38.0 %reduce-scatter.10.cloned.1.call-done = f32[192,768]{1,0:T(8,128)} async-done(((f32[768,768]{1,0:T(8,128)}), f32[192,768]{1,0:T(8,128)}) %reduce-scatter.10.cloned.1.call-update) | async-done | bytes 589840 | tf_op jit(solution)/shard_map/reduce_scatter | solution.py:240
  521.0 98.2 %reduce-scatter.12.cloned.1.call-done = f32[192,3072]{1,0:T(8,128)} async-done(((f32[768,3072]{1,0:T(8,128)}), f32[192,3072]{1,0:T(8,128)}) %reduce-scatter.12.cloned.1.call-update) | async-done | bytes 2359312 | tf_op jit(solution)/shard_map/reduce_scatter | solution.py:241
  619.1 98.2 %reduce-scatter.14.cloned.1.call-done = f32[768,768]{1,0:T(8,128)} async-done(((f32[3072,768]{1,0:T(8,128)}), f32[768,768]{1,0:T(8,128)}) %reduce-scatter.14.cloned.1.call-update) | async-done | bytes 2359312 | tf_op jit(solution)/shard_map/reduce_scatter | solution.py:242
  734.4 9.8 %add_bitcast_fusion = f32[1,1024,768]{1,2,0:T(8,128)} fusion(f32[1024,768]{0,1:T(8,128)} %copy-done.24, bf16[768,2304]{1,0:T(8,128)(2,1)} %all-gather.7.cloned.1.call-done, bf16[1024,768]{0,1:T(8,128)(2,1)} %bitcast.204, bf16[1024,768]{0,1:T(8,128)(2,1)} %bitcast.194, bf16[1024,768]{0,1:T(8,128)(2,1)} %bitcast.197), kind=kOutput, calls=%fused_computation.55 | convolution fusion | flops 3638820864 | bytes 14548992 | tf_op jit(solution)/shard_map/re,de->rd/dot_general | solution.py:216
  748.0 15.0 %all-reduce = f32[3072]{0:T(1024)S(1)} all-reduce(f32[3072]{0:T(1024)S(1)} %copy-done.44), channel_id=7, replica_groups=mesh['group'=4,'rep'=8] {'group'}, use_global_device_ids=true, to_apply=%region_31.32.clone | all-reduce | flops 3072 | bytes 24576
  764.1 28.1 %all-reduce.1 = (f32[192,8]{0,1:T(8,128)S(1)}, f32[768]{0:T(1024)S(1)}) all-reduce(f32[192,8]{0,1:T(8,128)S(1)} %copy.140, f32[768]{0:T(1024)S(1)} %dynamic-slice.1), channel_id=1, replica_groups=mesh['group'=4,'rep'=8] {'rep'}, use_global_device_ids=true, to_apply=%region_29.30 | all-reduce | flops 2304 | bytes 18432 | tf_op jit(solution)/shard_map/psum | solution.py:246
  794.7 117.2 %all-reduce.5.cloned.1.call-done = (f32[192,2304]{0,1:T(8,128)}, f32[192,768]{1,0:T(8,128)}, f32[192,3072]{1,0:T(8,128)}, f32[768,768]{1,0:T(8,128)}) async-done(((f32[192,2304]{0,1:T(8,128)}, f32[192,768]{1,0:T(8,128)}, f32[192,3072]{1,0:T(8,128)}, f32[768,768]{1,0:T(8,128)}), (f32[192,2304]{0,1:T(8,128)}, f32[192,768]{1,0:T(8,128)}, f32[192,3072]{1,0:T(8,128)}, ...) | async-done | bytes 7077904 | tf_op jit(solution)/shard_map/psum | solution.py:246
  (233 shorter events, 162.0 us)
Async XLA Ops:
  7.2 53.3 %all-gather.7.cloned.1.call-start = ((), (), s32[]{:S(2)}) async-start(), calls=%async_computation.5 | async-start | bytes 4423680 | tf_op jit(solution)/shard_map/all_gather | solution.py:129
  9.9 142.2 %all-gather.9.cloned.1.call-start = ((), (), s32[]{:S(2)}) async-start(), calls=%async_computation.6 | async-start | bytes 1474560 | tf_op jit(solution)/shard_map/all_gather | solution.py:130
  10.7 145.6 %all-gather.11.cloned.1.call-start = ((), (), s32[]{:S(2)}) async-start(), calls=%async_computation.7 | async-start | bytes 5898240 | tf_op jit(solution)/shard_map/all_gather | solution.py:131
  12.0 22.4 %copy-start.28 = (bf16[1,1024,768]{2,1,0:T(8,128)(2,1)S(1)}, bf16[1,1024,768]{2,1,0:T(8,128)(2,1)}, u32[]{:S(2)}) copy-start(bf16[1,1024,768]{2,1,0:T(8,128)(2,1)} %param.17) | copy-start | bytes 4718596
  12.0 197.6 %all-gather.13.cloned.1.call-start = ((), (), s32[]{:S(2)}) async-start(), calls=%async_computation.8 | async-start | bytes 5898240 | tf_op jit(solution)/shard_map/all_gather | solution.py:132
  15.0 21.0 %copy-start.29 = (bf16[1,1024,768]{2,1,0:T(8,128)(2,1)S(1)}, bf16[1,1024,768]{2,1,0:T(8,128)(2,1)}, u32[]{:S(2)}) copy-start(bf16[1,1024,768]{2,1,0:T(8,128)(2,1)} %param.16) | copy-start | bytes 4718596
  15.0 465.1 %reduce-scatter.16.cloned.1.call-start = ((), (), s32[]{:S(2)}) async-start(), calls=%async_computation.12 | async-start | bytes 8847360
  34.1 175.5 %copy-start.46 = (f32[768]{0:T(1024)}, f32[768]{0:T(1024)S(1)}, u32[]{:S(2)}) copy-start(f32[768]{0:T(1024)S(1)} %get-tuple-element.162) | copy-start | bytes 9220
  38.4 80.9 %copy-start = (pred[1024,1024]{0,1:T(8,128)(4,1)}, pred[1024,1024]{0,1:T(8,128)(4,1)S(1)}, u32[]{:S(2)}) copy-start(pred[1024,1024]{0,1:T(8,128)(4,1)S(1)} %bitcast_and_fusion) | copy-start | bytes 3145732
  96.9 22.4 %copy-start.21 = (bf16[1024,768]{0,1:T(8,128)(2,1)S(1)}, bf16[1024,768]{0,1:T(8,128)(2,1)}, u32[]{:S(2)}) copy-start(bf16[1024,768]{0,1:T(8,128)(2,1)} %copy.109) | copy-start | bytes 4718596
  155.9 38.8 %copy-start.7 = (f32[1024,768]{0,1:T(8,128)}, f32[1024,768]{0,1:T(8,128)S(1)}, u32[]{:S(2)}) copy-start(f32[1024,768]{0,1:T(8,128)S(1)} %get-tuple-element.207) | copy-start | bytes 9437188
  156.4 53.3 %copy-start.48 = (f32[768]{0:T(1024)S(1)}, f32[768]{0:T(1024)}, u32[]{:S(2)}) copy-start(f32[768]{0:T(1024)} %get-tuple-element.161) | copy-start | bytes 9220
  219.5 24.1 %copy-start.2 = (f32[1024,768]{0,1:T(8,128)}, f32[1024,768]{0,1:T(8,128)S(1)}, u32[]{:S(2)}) copy-start(f32[1024,768]{0,1:T(8,128)S(1)} %get-tuple-element.210) | copy-start | bytes 9437188
  316.4 41.2 %copy-start.6 = (bf16[1024,768]{0,1:T(8,128)(2,1)S(1)}, bf16[1024,768]{0,1:T(8,128)(2,1)}, u32[]{:S(2)}) copy-start(bf16[1024,768]{0,1:T(8,128)(2,1)} %copy-done.5) | copy-start | bytes 4718596
  403.1 117.8 %reduce-scatter.10.cloned.1.call-start = ((), (), s32[]{:S(2)}) async-start(), calls=%async_computation.9 | async-start | bytes 2949120 | tf_op jit(solution)/shard_map/reduce_scatter | solution.py:240
  408.6 210.6 %reduce-scatter.12.cloned.1.call-start = ((), (), s32[]{:S(2)}) async-start(), calls=%async_computation.10 | async-start | bytes 11796480 | tf_op jit(solution)/shard_map/reduce_scatter | solution.py:241
  420.6 296.7 %reduce-scatter.14.cloned.1.call-start = ((), (), s32[]{:S(2)}) async-start(), calls=%async_computation.11 | async-start | bytes 11796480 | tf_op jit(solution)/shard_map/reduce_scatter | solution.py:242
  433.3 329.8 %reduce-scatter.18.cloned.1.call-start = ((), (), s32[]{:S(2)}) async-start(), calls=%async_computation.13 | async-start | bytes 491520
  440.3 471.5 %all-reduce.5.cloned.1.call-start = ((), (), s32[]{:S(2)}) async-start(), calls=%async_computation.14 | async-start | bytes 15335424 | tf_op jit(solution)/shard_map/psum | solution.py:246
  744.2 47.9 %copy-start.43 = (f32[768]{0:T(1024)S(1)}, f32[768]{0:T(1024)}, u32[]{:S(2)}) copy-start(f32[768]{0:T(1024)} %param.25) | copy-start | bytes 9220
  744.2 49.2 %copy-start.34 = (f32[2,192,8]{1,2,0:T(8,128)S(1)}, f32[2,192,8]{1,2,0:T(8,128)}, u32[]{:S(2)}) copy-start(f32[2,192,8]{1,2,0:T(8,128)} %param.30) | copy-start | bytes 36868
  744.2 49.8 %copy-start.37 = (f32[192,8]{0,1:T(8,128)S(1)}, f32[192,8]{0,1:T(8,128)}, u32[]{:S(2)}) copy-start(f32[192,8]{0,1:T(8,128)} %param.24) | copy-start | bytes 18436
  744.3 167.6 %copy-start.11 = (f32[192,2304]{0,1:T(8,128)S(1)}, f32[192,2304]{0,1:T(8,128)}, u32[]{:S(2)}) copy-start(f32[192,2304]{0,1:T(8,128)} %copy.124) | copy-start | bytes 5308420
  793.4 125.5 %copy-start.38 = (f32[192,8]{0,1:T(8,128)}, f32[192,8]{0,1:T(8,128)S(1)}, u32[]{:S(2)}) copy-start(f32[192,8]{0,1:T(8,128)S(1)} %get-tuple-element.176) | copy-start | bytes 18436
  (45 other events, 221.1 us)
Sparse Core Ops, SparseCore 0:
  10.5 50.0 all-gather.6
  62.9 27.7 all-gather.8
  93.1 57.0 all-gather.10
  152.5 57.0 all-gather.12
  403.2 76.7 reduce-scatter.15
  483.5 37.3 reduce-scatter.9
  524.1 95.0 reduce-scatter.11
  622.2 95.0 reduce-scatter.13
  720.7 24.4 reduce-scatter.17
  748.2 163.6 all-reduce.4
where the time goes:
time: 970 us; the launch traced here: 961 us
  waiting for transfers between devices  428 us (44%)
  matrix products  275 us (28%)
  other arithmetic  116 us (12%)
  local copies, waits for them, and re-layouts  64.3 us (7%)
  blocking collectives  61.2 us (6%)
  between operations  15.7 us (2%)
    psum x1, waiting for transfers between devices, local(): lax.psum((shard_qkv, shard_out, shard_in, shard_down, shard_vec, shard_bi...  117 us
    reduce_scatter x1, waiting for transfers between devices, local(): lax.psum_scatter(grad_w_in, 'group', scatter_dimension=0, tiled=True)  98.2 us
    reduce_scatter x1, waiting for transfers between devices, local(): lax.psum_scatter(grad_w_down, 'group', scatter_dimension=0, tiled=True)  98.2 us
    unnamed x136, local copies, waits for them, and re-layouts  50.2 us
    convert_element_type x1, other arithmetic, attend_backward(): (attention_weights_soft * (probability_gradient - inner_sum)).astype(jnp....  41.1 us
    unnamed x12, waiting for transfers between devices  39.8 us
    dot_general x1, matrix products, local(): jnp.dot(first_low, full_in, preferred_element_type=jnp.float32) + bias_full  38.3 us
    reduce_scatter x1, waiting for transfers between devices, local(): lax.psum_scatter(grad_w_out, 'group', scatter_dimension=0, tiled=True)  38 us
  transfers between devices with their start and end apart: 10, of which 7 were waited for; matrix products, arithmetic and copies ran while one was open for 22% of the time, Pallas kernels for 0%

commit v1 on v0

v1 whole, which is shorter than its diff:
```python
import jax
import jax.numpy as jnp
from jax import lax
from jax.experimental import pallas as pl
from jax.experimental.pallas import tpu as pltpu
from jax.sharding import PartitionSpec as P

HEAD_DIM = 64
STEP = 4
norm_eps = 1e-05
adam_eps = 1e-08
matrix_decay = 0.1
step_rate = 0.1
BF = jnp.bfloat16
F32 = jnp.float32
I32 = jnp.int32
VM = 56 * 1024 * 1024
NEG = -1e30
PAIR = 2 * HEAD_DIM
SQH = 0.7071067811865476
PHI0 = 0.3989422804014327
AX = ("group", "rep")
ANY = pl.BlockSpec(memory_space=pl.ANY)
SMEM = pl.BlockSpec(memory_space=pltpu.SMEM)
VMEM = pl.BlockSpec(memory_space=pltpu.VMEM)
sds = jax.ShapeDtypeStruct


def cost(flops, nbytes, trans=0):
    return pl.CostEstimate(flops=int(flops), bytes_accessed=int(nbytes), transcendentals=int(trans))


def params(**kw):
    return pltpu.CompilerParams(vmem_limit_bytes=VM, **kw)

def nt(a, b):
    return lax.dot_general(a, b, (((1,), (1,)), ((), ())), preferred_element_type=F32)


def nn(a, b):
    return lax.dot_general(a, b, (((1,), (0,)), ((), ())), preferred_element_type=F32)


def tn(a, b):
    return lax.dot_general(a, b, (((0,), (0,)), ((), ())), preferred_element_type=F32)


def split3(v):
    hi = v.astype(BF).astype(F32)
    mid = (v - hi).astype(BF).astype(F32)
    return hi, mid, v - hi - mid


def attn_feats(seg_ref, rand_ref, fq_s, fk_s, nb):
    n = fq_s.shape[0]
    bl = n // nb
    lane = lax.broadcasted_iota(jnp.int32, (n, PAIR), 1) % HEAD_DIM
    blk = lax.broadcasted_iota(jnp.int32, (n, PAIR), 0) // bl
    seg = seg_ref[...]
    fq = (lane == blk) | ((lane >= nb) & (lane - nb == seg))
    fq_s[...] = jnp.where(fq, 1.0, 0.0).astype(BF)
    allow = (jnp.abs(lane - blk) <= 1) | (lane == 0) | (lane == nb - 1) | (blk == 0) | (blk == nb - 1)
    for j in range(rand_ref.shape[0]):
        allow = allow | (rand_ref[j : j + 1, :] == blk)
    bad = ((lane < nb) & jnp.logical_not(allow)) | ((lane >= nb) & (lane < nb + 4) & (lane - nb != seg))
    off = (lane >= nb + 4) & (lane < nb + 7)
    fk_s[...] = jnp.where(bad, NEG, jnp.where(off, -1.0, 0.0)).astype(BF)


def attn_fwd_kernel(nb, seg_ref, rand_ref, q_ref, k_ref, v_ref, o_ref, f_ref, fq_s, fk_s):
    @pl.when(pl.program_id(0) == 0)
    def _():
        attn_feats(seg_ref, rand_ref, fq_s, fk_s, nb)

    n = q_ref.shape[0]
    t = 256
    low1 = lax.broadcasted_iota(jnp.int32, (n, PAIR), 1) < HEAD_DIM
    k = k_ref[...]
    v = v_ref[...]
    fk = fk_s[...]
    one = jnp.ones((n, PAIR), BF)
    ks = (jnp.where(low1, k, fk), jnp.where(low1, fk, k))
    vs = (jnp.where(low1, v, one), jnp.where(low1, one, v))
    lowt = lax.broadcasted_iota(jnp.int32, (t, PAIR), 1) < HEAD_DIM
    lane = lax.broadcasted_iota(jnp.int32, (t, PAIR), 1) % HEAD_DIM
    for i in range(n // t):
        rows = pl.ds(i * t, t)
        q = q_ref[rows, :] * jnp.asarray(HEAD_DIM**-0.5, BF)
        fq = fq_s[rows, :]
        acc, top = [], []
        for h in range(2):
            qh = jnp.where(lowt, q, fq) if h == 0 else jnp.where(lowt, fq, q)
            s = nt(qh, ks[h])
            m = jnp.max(s, axis=-1, keepdims=True)
            p = jnp.exp(s - m).astype(BF)
            acc.append(nn(p, vs[h]))
            top.append(m)
        lsw = jnp.where(lowt, acc[1], acc[0])
        o = jnp.where(lowt, acc[0], acc[1]) / pltpu.roll(lsw, HEAD_DIM, 1)
        o_ref[rows, :] = o.astype(BF)
        hi, mid, lo = split3(jnp.where(lowt, top[1], top[0]) + jnp.log(lsw))
        f = jnp.where(lane == nb + 4, hi, jnp.where(lane == nb + 5, mid, lo))
        f_ref[rows, :] = jnp.where((lane >= nb + 4) & (lane < nb + 7), f.astype(BF), fq)


def attn_fwd(qkv, seg_col, rand_rows, nb):
    n, w3 = qkv.shape
    w = w3 // 3
    pairs = w // PAIR
    blk = lambda off: pl.BlockSpec((n, PAIR), lambda p, off=off: (0, p + off))
    full = lambda a: pl.BlockSpec(a.shape, lambda p: (0, 0))
    return pl.pallas_call(
        lambda *refs: attn_fwd_kernel(nb, *refs),
        grid=(pairs,),
        in_specs=[full(seg_col), full(rand_rows), blk(0), blk(pairs), blk(2 * pairs)],
        out_specs=[blk(0), blk(0)],
        out_shape=[jax.ShapeDtypeStruct((n, w), BF)] * 2,
        scratch_shapes=[pltpu.VMEM((n, PAIR), BF)] * 2,
        compiler_params=pltpu.CompilerParams(vmem_limit_bytes=VM),
        name="attn_fwd",
    )(seg_col, rand_rows, qkv, qkv, qkv)


def attn_bwd_kernel(nb, seg_ref, rand_ref, q_ref, k_ref, v_ref, f_ref, o_ref, do_ref, dq_ref, dk_ref, dv_ref, bias_ref, fq_s, fk_s):
    @pl.when(pl.program_id(0) == 0)
    def _():
        attn_feats(seg_ref, rand_ref, fq_s, fk_s, nb)

    n = q_ref.shape[0]
    t = 256
    low1 = lax.broadcasted_iota(jnp.int32, (n, PAIR), 1) < HEAD_DIM
    lane = lax.broadcasted_iota(jnp.int32, (n, PAIR), 1) % HEAD_DIM
    scale = jnp.asarray(HEAD_DIM**-0.5, BF)
    q = q_ref[...] * scale
    f = f_ref[...]
    do = do_ref[...]
    prod = do.astype(F32) * o_ref[...].astype(F32)
    d0 = jnp.sum(jnp.where(low1, prod, 0.0), axis=-1, keepdims=True)
    d1 = jnp.sum(jnp.where(low1, 0.0, prod), axis=-1, keepdims=True)
    hi, mid, lo = split3(jnp.where(low1, d1, d0))
    fd = jnp.where(lane == nb + 4, hi, jnp.where(lane == nb + 5, mid, jnp.where(lane == nb + 6, lo, 0.0))).astype(BF)
    qs = (jnp.where(low1, q, f), jnp.where(low1, f, q))
    dos = (jnp.where(low1, do, fd), jnp.where(low1, fd, do))
    kT = jnp.transpose(k_ref[...] * scale)
    lowt = lax.broadcasted_iota(jnp.int32, (t, PAIR), 1) < HEAD_DIM
    dqT = [None, None]
    dv_sum = jnp.zeros((1, PAIR), F32)
    for i in range(n // t):
        rows = pl.ds(i * t, t)
        k = k_ref[rows, :]
        v = v_ref[rows, :]
        fk = fk_s[rows, :]
        fv = jnp.where(fk == -1.0, fk, jnp.zeros_like(fk))
        dvh, dkh = [], []
        for h in range(2):
            kh = jnp.where(lowt, k, fk) if h == 0 else jnp.where(lowt, fk, k)
            vh = jnp.where(lowt, v, fv) if h == 0 else jnp.where(lowt, fv, v)
            p = jnp.exp(nt(kh, qs[h]))
            ds = (p * nt(vh, dos[h])).astype(BF)
            dvh.append(nn(p.astype(BF), do))
            dkh.append(nn(ds, q))
            part = nn(kT[h * HEAD_DIM : (h + 1) * HEAD_DIM, i * t : (i + 1) * t], ds)
            dqT[h] = part if dqT[h] is None else dqT[h] + part
        dk_ref[rows, :] = jnp.where(lowt, dkh[0], dkh[1]).astype(BF)
        dv = jnp.where(lowt, dvh[0], dvh[1]).astype(BF)
        dv_ref[rows, :] = dv
        dv_sum = dv_sum + jnp.sum(dv.astype(F32), axis=0, keepdims=True)
    dq = jnp.transpose(jnp.concatenate(dqT, axis=0)).astype(BF)
    dq_ref[...] = dq
    bias_ref[...] = jnp.concatenate([jnp.sum(dq.astype(F32), axis=0, keepdims=True), dv_sum, jnp.zeros((6, PAIR), F32)], axis=0)


def attn_bwd(qkv, f, o, do, seg_col, rand_rows, nb):
    n, w3 = qkv.shape
    w = w3 // 3
    pairs = w // PAIR
    blk = lambda off: pl.BlockSpec((n, PAIR), lambda p, off=off: (0, p + off))
    full = lambda a: pl.BlockSpec(a.shape, lambda p: (0, 0))
    return pl.pallas_call(
        lambda *refs: attn_bwd_kernel(nb, *refs),
        grid=(pairs,),
        in_specs=[full(seg_col), full(rand_rows), blk(0), blk(pairs), blk(2 * pairs), blk(0), blk(0), blk(0)],
        out_specs=[blk(0), blk(0), blk(0), pl.BlockSpec((8, PAIR), lambda p: (0, p))],
        out_shape=[jax.ShapeDtypeStruct((n, w), BF)] * 3 + [jax.ShapeDtypeStruct((8, w), F32)],
        scratch_shapes=[pltpu.VMEM((n, PAIR), BF)] * 2,
        compiler_params=pltpu.CompilerParams(vmem_limit_bytes=VM),
        name="attn_bwd",
    )(seg_col, rand_rows, qkv, qkv, qkv, f, o, do)


def norm(r, g, c):
    w = r.shape[-1]
    center = r - jnp.sum(r, axis=-1, keepdims=True) * (1.0 / w)
    inv = lax.rsqrt(jnp.sum(center * center, axis=-1, keepdims=True) * (1.0 / w) + norm_eps)
    n = center * inv
    return n * g + c, n, inv


def norm_back(dy, g, n, inv):
    w = dy.shape[-1]
    e = dy * g
    a = jnp.sum(e, axis=-1, keepdims=True) * (1.0 / w)
    b = jnp.sum(e * n, axis=-1, keepdims=True) * (1.0 / w)
    return inv * (e - a - n * b)


def colsum(a):
    return jnp.sum(a, axis=0, keepdims=True)


def pack_a(where, w, vec_t, bias):
    rows, cols = w.shape
    half = rows // 2

    def kern(where_ref, w_ref, vec_ref, bias_ref, out_ref):
        for h in range(2):
            pos = h ^ where_ref[1]
            out_ref[pos, 0:half, :] = w_ref[h * half : (h + 1) * half, :].astype(BF)
            small = vec_ref[...] if h == 0 else bias_ref[...]
            small = jnp.concatenate([small, jnp.zeros((small.shape[0], cols - small.shape[1]), F32)], axis=1)
            out_ref[pos, half : half + 16, :] = jnp.concatenate([small, small], axis=0).astype(BF)

    return pl.pallas_call(
        kern,
        in_specs=[SMEM, VMEM, VMEM, VMEM],
        out_specs=VMEM,
        out_shape=sds((2, half + 16, cols), BF),
        compiler_params=params(),
        cost_estimate=cost(0, 3 * w.size * 2),
        name="pack_a",
    )(where, w, vec_t, bias)


def pack_b(where, wo, wi, wd):
    rows, w = wo.shape
    half = rows // 2
    nf = wi.shape[1] // w
    nd = wd.shape[0] // rows

    def kern(where_ref, wo_ref, wi_ref, wd_ref, out_ref):
        for h in range(2):
            pos = h ^ where_ref[1]
            hs = slice(h * half, (h + 1) * half)
            out_ref[pos, 0] = wo_ref[hs, :].astype(BF)
            for j in range(nf):
                out_ref[pos, 1 + j] = wi_ref[hs, j * w : (j + 1) * w].astype(BF)
            for j in range(nd):
                at = (h * nd + j) * half
                out_ref[pos, 1 + nf + j] = wd_ref[at : at + half, :].astype(BF)

    return pl.pallas_call(
        kern,
        in_specs=[SMEM, VMEM, VMEM, VMEM],
        out_specs=VMEM,
        out_shape=sds((2, 1 + nf + nd, half, w), BF),
        compiler_params=params(),
        cost_estimate=cost(0, 6 * (wo.size + wi.size + wd.size)),
        name="pack_b",
    )(where, wo, wi, wd)


def pperm(a, pairs):
    return lax.ppermute(a, AX, pairs)


def gather(pack, perms):
    near = pperm(pack, perms["s1"])
    side = pperm(near, perms["core"])
    far = pperm(near[0:1], perms["s2"])
    back = pperm(far, perms["core"])
    return pack, near, side, far, back


def piece_refs(refs):
    own, near, side, far, back = refs
    return [own.at[0], own.at[1], near.at[0], near.at[1], side.at[0], side.at[1], far.at[0], back.at[0]]


def project(x, table, parts, groups, t=256):
    n, d = x.shape
    _, hp, cols = parts[0].shape
    half = hp - 16
    share = 2 * half

    def kern(tab_ref, x_ref, *refs):
        pieces = piece_refs(refs[:5])
        qkv_ref, w_out, vec_ref, bias_ref, w_s, e_s, sems, osem = refs[5:]
        first = pl.program_id(0) == 0
        last = pl.program_id(0) == pl.num_programs(0) - 1

        def copies():
            out = []
            for i, p in enumerate(pieces):
                u = tab_ref[i]
                out.append(pltpu.make_async_copy(p.at[pl.ds(0, half)], w_s.at[pl.ds(pl.multiple_of(u * half, 16), half)], sems.at[2 * i]))
                out.append(pltpu.make_async_copy(p.at[pl.ds(half, 16)], e_s.at[u], sems.at[2 * i + 1]))
            return out

        def whole():
            return pltpu.make_async_copy(w_s, w_out, osem)

        @pl.when(first)
        def _():
            for cp in copies():
                cp.start()
            for cp in copies():
                cp.wait()
            whole().start()
            vec_ref[...] = jnp.concatenate([e_s[2 * g, 0:8, 0:share].astype(F32) for g in range(groups)], axis=1)
            for g in range(groups):
                bias_ref[g] = e_s[2 * g + 1, 0:8, 0:d].astype(F32)

        qb = jnp.concatenate([vec_ref[0:1, :], jnp.zeros((1, d), F32), vec_ref[1:2, :]], axis=1)
        qkv_ref[...] = (nn(x_ref[...], w_s[...]) + qb).astype(BF)

        @pl.when(last)
        def _():
            whole().wait()

    return pl.pallas_call(
        kern,
        grid=(n // t,),
        in_specs=[SMEM, pl.BlockSpec((t, d), lambda i: (i, 0))] + [ANY] * 5,
        out_specs=[pl.BlockSpec((t, cols), lambda i: (i, 0)), ANY, pl.BlockSpec((8, d), lambda i: (0, 0)), pl.BlockSpec((groups, 8, d), lambda i: (0, 0, 0))],
        out_shape=[sds((n, cols), BF), sds((d, cols), BF), sds((8, d), F32), sds((groups, 8, d), F32)],
        scratch_shapes=[pltpu.VMEM((d, cols), BF), pltpu.VMEM((2 * groups, 16, cols), BF), pltpu.SemaphoreType.DMA((16,)), pltpu.SemaphoreType.DMA],
        compiler_params=params(),
        cost_estimate=cost(2 * n * d * cols, 2 * (n * d + 2 * d * cols + n * cols)),
        name="project",
    )(table, x, *parts)


def token(x, dy, o, vec, bias, table, parts, t=256):
    n, w = x.shape
    _, k9, half, _ = parts[0].shape
    nf = bias.shape[0]
    nd = k9 - 1 - nf
    ff = nf * w

    def kern(tab_ref, x_ref, dy_ref, o_ref, vec_ref, bias_ref, *refs):
        pieces = piece_refs(refs[:5])
        (y_ref, dr1_ref, hb_ref, dh_ref, x1b_ref, dfb_ref, dab_ref, do_ref, vs_ref, bs_ref, wo_s, wi_s, wd_s, sems) = refs[5:]
        first = pl.program_id(0) == 0

        def copies(kind):
            out = []
            for i, p in enumerate(pieces):
                u = tab_ref[i]
                rows = pl.ds(pl.multiple_of(u * half, 16), half)
                if kind == 0:
                    out.append(pltpu.make_async_copy(p.at[0], wo_s.at[rows], sems.at[0, i]))
                elif kind == 1:
                    out.append(pltpu.make_async_copy(p.at[pl.ds(1, nf)], wi_s.at[:, rows], sems.at[1, i]))
                else:
                    out.append(pltpu.make_async_copy(p.at[pl.ds(1 + nf, nd)], wd_s.at[pl.ds(u * nd, nd)], sems.at[2, i]))
            return out

        @pl.when(first)
        def _():
            for kind in range(3):
                for cp in copies(kind):
                    cp.start()
            for kind in range(3):
                for cp in copies(kind):
                    cp.wait()

        row = lambda j: vec_ref[j : j + 1, :]
        bo, g1, c1, bd, g2, c2 = [row(j) for j in range(2, 8)]
        per = wd_s.shape[0] // nf
        down = lambda j: wd_s[j * per : (j + 1) * per].reshape(w, w)
        xf = x_ref[...].astype(F32)
        x1, n1, inv1 = norm(xf + (nn(o_ref[...], wo_s[...]) + bo), g1, c1)
        x1b = x1.astype(BF)
        x1b_ref[...] = x1b
        back = None
        slopes = []
        for j in range(nf):
            cols = slice(j * w, (j + 1) * w)
            h = nn(x1b, wi_s[j]) + bias_ref[j, 0:1, :]
            cdf = 0.5 * (1.0 + lax.erf(h * SQH))
            hb = (h * cdf).astype(BF)
            slopes.append(cdf + h * (jnp.exp(-0.5 * (h * h)) * PHI0))
            hb_ref[:, cols] = hb
            part = nn(hb, down(j))
            back = part if back is None else back + part
        y, n2, inv2 = norm(x1 + (back + bd), g2, c2)
        y_ref[...] = y
        dyf = dy_ref[...].astype(F32)
        dr2 = norm_back(dyf, g2, n2, inv2)
        dfb = dr2.astype(BF)
        dfb_ref[...] = dfb
        dx1 = dr2
        bsum = []
        for j in range(nf):
            cols = slice(j * w, (j + 1) * w)
            dh = (nt(dfb, down(j)) * slopes[j]).astype(BF)
            dh_ref[:, cols] = dh
            bsum.append(colsum(dh.astype(F32)))
            dx1 = dx1 + nt(dh, wi_s[j])
        dr1 = norm_back(dx1, g1, n1, inv1)
        dr1_ref[...] = dr1
        dab = dr1.astype(BF)
        dab_ref[...] = dab
        do_ref[...] = nt(dab, wo_s[...]).astype(BF)
        zero = jnp.zeros((2, w), F32)
        vsum = jnp.concatenate([zero, colsum(dr1), colsum(dx1 * n1), colsum(dx1), colsum(dr2), colsum(dyf * n2), colsum(dyf)], axis=0)
        bsum = jnp.concatenate(bsum + [jnp.zeros((8 - nf, w), F32)], axis=0)
        vs_ref[...] = vsum + jnp.where(first, 0.0, vs_ref[...])
        bs_ref[...] = bsum + jnp.where(first, 0.0, bs_ref[...])

    rows = lambda c: pl.BlockSpec((t, c), lambda i: (i, 0))
    full = lambda s: pl.BlockSpec(s, lambda i: (0,) * len(s))
    return pl.pallas_call(
        kern,
        grid=(n // t,),
        in_specs=[SMEM, rows(w), rows(w), rows(w), full(vec.shape), full(bias.shape)] + [ANY] * 5,
        out_specs=[rows(w), rows(w), rows(ff), rows(ff), rows(w), rows(w), rows(w), rows(w), full((8, w)), full((8, w))],
        out_shape=[sds((n, w), F32), sds((n, w), F32), sds((n, ff), BF), sds((n, ff), BF)] + [sds((n, w), BF)] * 4 + [sds((8, w), F32), sds((8, w), F32)],
        scratch_shapes=[pltpu.VMEM((w, w), BF), pltpu.VMEM((nf, w, w), BF), pltpu.VMEM((ff // half, half, w), BF), pltpu.SemaphoreType.DMA((3, 8))],
        compiler_params=params(),
        cost_estimate=cost(2 * n * w * (2 * w + 4 * ff), 2 * (n * (9 * w + 2 * ff) + w * (w + 2 * ff)), 2 * n * ff),
        name="token",
    )(table, x, dy, o, vec, bias, *parts)


def grad_down(order, half, hb, dfb, groups, quarters):
    n, ff = hb.shape
    w = dfb.shape[1]
    share = ff // groups
    hr = share // 2
    rb = hr // quarters

    def kern(order_ref, half_ref, hb_ref, dfb_ref, out_ref):
        g = pl.program_id(0)
        r = tn(hb_ref[...], dfb_ref[...])
        for q in range(quarters):
            out_ref[order_ref[g * quarters + q]] = r[q * rb : (q + 1) * rb].astype(BF)

    return pl.pallas_call(
        kern,
        grid_spec=pltpu.PrefetchScalarGridSpec(
            num_scalar_prefetch=2,
            grid=(groups,),
            in_specs=[pl.BlockSpec((n, hr), lambda g, o, h: (0, 2 * g + h[0])), pl.BlockSpec((n, w), lambda g, o, h: (0, 0))],
            out_specs=pl.BlockSpec((groups * quarters, rb, w), lambda g, o, h: (0, 0, 0)),
        ),
        out_shape=sds((groups * quarters, rb, w), BF),
        compiler_params=params(),
        cost_estimate=cost(n * ff * w, 2 * (n * ff // 2 + n * w + ff * w // 2)),
        name="grad_down",
    )(order, half, hb, dfb)


def grad_cols(order, half, pairs, blocks, small, name):
    n, d = pairs[0][0].shape
    rb = d // blocks
    widths = [b.shape[1] // 2 for _, b in pairs]
    unit = min(widths)
    pieces = sum(widths) // unit
    rows = pieces * rb + (0 if small is None else 16)
    lefts = []
    for a, _ in pairs:
        if not any(a is b for b in lefts):
            lefts.append(a)
    where = [next(i for i, l in enumerate(lefts) if l is a) for a, _ in pairs]

    def kern(order_ref, half_ref, *refs):
        a_refs, b_refs, rest = refs[: len(lefts)], refs[len(lefts) : len(lefts) + len(pairs)], refs[len(lefts) + len(pairs) :]
        out_ref = rest[-1]
        at = 0
        for i in range(len(pairs)):
            r = tn(a_refs[where[i]][...], b_refs[i][...]).astype(BF)
            for j in range(widths[i] // unit):
                for k in range(blocks):
                    out_ref[order_ref[k], at : at + rb, :] = r[k * rb : (k + 1) * rb, j * unit : (j + 1) * unit]
                at += rb
        if small is not None:
            for k in range(blocks):
                row = rest[0][k, pl.ds(half_ref[0], 1), :]
                out_ref[order_ref[k], at : at + 16, :] = jnp.broadcast_to(row, (16, unit)).astype(BF)

    full = lambda s: pl.BlockSpec(s, lambda i, o, h: (0,) * len(s))
    out = (blocks, rows, unit)
    extra = [] if small is None else [small]
    return pl.pallas_call(
        kern,
        grid_spec=pltpu.PrefetchScalarGridSpec(
            num_scalar_prefetch=2,
            grid=(1,),
            in_specs=[full(a.shape) for a in lefts]
            + [pl.BlockSpec((n, wd), lambda i, o, h: (0, h[0])) for wd in widths]
            + [full(s.shape) for s in extra],
            out_specs=full(out),
        ),
        out_shape=sds(out, BF),
        compiler_params=params(),
        cost_estimate=cost(2 * n * d * sum(widths), 2 * (n * d + n * sum(widths) + d * sum(widths))),
        name=name,
    )(order, half, *lefts, *[b for _, b in pairs], *extra)


def grad_input(dr1, dq, dk, dv, w, t=256):
    n, d = dr1.shape

    def kern(r_ref, q_ref, k_ref, v_ref, w_ref, out_ref):
        out_ref[...] = r_ref[...] + nt(q_ref[...], w_ref[:, 0:d]) + nt(k_ref[...], w_ref[:, d : 2 * d]) + nt(v_ref[...], w_ref[:, 2 * d : 3 * d])

    rows = pl.BlockSpec((t, d), lambda i: (i, 0))
    return pl.pallas_call(
        kern,
        grid=(n // t,),
        in_specs=[rows] * 4 + [pl.BlockSpec(w.shape, lambda i: (0, 0))],
        out_specs=rows,
        out_shape=sds((n, d), F32),
        compiler_params=params(),
        cost_estimate=cost(6 * n * d * d, n * d * 14 + 2 * w.size),
        name="grad_input",
    )(dr1, dq, dk, dv, w)


def total(*terms):
    out = terms[0].astype(F32)
    for a in terms[1:]:
        out = out + a.astype(F32)
    return out.astype(BF)


def reduce_all(send, keep, perms):
    nb = keep.shape[0]
    a, b = nb // 2, nb // 4
    got = pperm(send, perms["core"])
    x1 = pperm(total(keep[a:], got[a:]), perms["s1"])
    x2 = pperm(total(keep[b:a], got[b:a], x1[b:]), perms["s2"])
    k, g, x = keep[:b], got[:b], x1[:b]
    m, e = b // 2, b // 4
    z1 = pperm(total(k[m:], g[m:], x[m:], x2[m:]), perms["z1"])
    z2 = pperm(total(k[e:m], g[e:m], x[e:m], x2[e:m], z1[e:]), perms["z2"])
    t0 = total(k[:e], g[:e], x[:e], x2[:e], z1[:e], z2)
    for extra in perms["far"]:
        t0 = total(t0, pperm(t0, extra))
    t1 = pperm(t0, perms["z2"])
    t01 = jnp.concatenate([t0, t1], axis=0)
    t23 = pperm(t01, perms["z1"])
    return t01, t23, pperm(t01, perms["core"]), pperm(t23, perms["core"])


def adam(w, m, u, g, decay):
    correct = 1.0 - 0.5**STEP
    m = 0.5 * m + 0.5 * g
    u = 0.5 * u + 0.5 * g * g
    return w - step_rate * (m / correct / (jnp.sqrt(u / correct) + adam_eps) + decay * w), m, u


def pick(lo_ref, hi_ref, t, rows=slice(None)):
    lo = lo_ref[t % 2, rows, :].astype(F32)
    hi = hi_ref[t % 2, rows, :].astype(F32)
    return jnp.where(t < 2, lo, hi)


def adam_down(where, tabs, sums, w, mom, count):
    rows, cols = w.shape
    rb = rows // 8

    def kern(where_ref, tab_ref, a0, a1, b0, b1, w_ref, m_ref, g_out, w_out, m_out):
        i = pl.program_id(0)
        mine = i // 4 == where_ref[1]
        q = i % 4
        g = jnp.where(mine, pick(a0, a1, tab_ref[q]), pick(b0, b1, tab_ref[4 + q])) * count
        g_out[...] = g
        w_out[...], m_out[0], m_out[1] = adam(w_ref[...], m_ref[0], m_ref[1], g, matrix_decay)

    full = lambda s: pl.BlockSpec(s, lambda i: (0,) * len(s))
    blk = pl.BlockSpec((rb, cols), lambda i: (i, 0))
    blk2 = pl.BlockSpec((2, rb, cols), lambda i: (0, i, 0))
    return pl.pallas_call(
        kern,
        grid=(8,),
        in_specs=[SMEM, SMEM] + [full(s.shape) for s in sums] + [blk, blk2],
        out_specs=[blk, blk, blk2],
        out_shape=[sds(w.shape, F32), sds(w.shape, F32), sds(mom.shape, F32)],
        compiler_params=params(),
        cost_estimate=cost(20 * w.size, 28 * w.size, 2 * w.size),
        name="adam_down",
    )(where, tabs, *sums, w, mom)


def adam_cols(where, tabs, sums, mats, at, count, name):
    unit = sums[0].shape[2]
    k = len(mats)

    def kern(where_ref, tab_ref, a0, a1, b0, b1, *refs):
        q = pl.program_id(0)
        flip = where_ref[1] == 1
        ta, tb = tab_ref[q], tab_ref[4 + q]
        p = at
        for i, (w, _, parts, per) in enumerate(mats):
            w_ref, m_ref = refs[2 * i], refs[2 * i + 1]
            g_out, w_out, m_out = refs[2 * k + 3 * i : 2 * k + 3 * i + 3]
            rb = w.shape[0] // 4
            for part in range(parts):
                for j in range(per):
                    rows = slice(p, p + rb)
                    a, b = pick(a0, a1, ta, rows) * count, pick(b0, b1, tb, rows) * count
                    p += rb
                    for h in range(2):
                        g = jnp.where(flip, b, a) if h == 0 else jnp.where(flip, a, b)
                        c0 = ((part * 2 + h) * per + j) * unit
                        cs = slice(c0, c0 + unit)
                        g_out[:, cs] = g
                        w_out[:, cs], m_out[0, :, cs], m_out[1, :, cs] = adam(w_ref[:, cs], m_ref[0, :, cs], m_ref[1, :, cs], g, matrix_decay)

    full = lambda s: pl.BlockSpec(s, lambda i: (0,) * len(s))
    ins, outs, shapes, args = [], [], [], []
    for w, mom, _, _ in mats:
        blk = pl.BlockSpec((w.shape[0] // 4, w.shape[1]), lambda i: (i, 0))
        blk2 = pl.BlockSpec((2, w.shape[0] // 4, w.shape[1]), lambda i: (0, i, 0))
        ins += [blk, blk2]
        outs += [blk, blk, blk2]
        shapes += [sds(w.shape, F32), sds(w.shape, F32), sds(mom.shape, F32)]
        args += [w, mom]
    size = sum(w.size for w, _, _, _ in mats)
    return pl.pallas_call(
        kern,
        grid=(4,),
        in_specs=[SMEM, SMEM] + [full(s.shape) for s in sums] + ins,
        out_specs=outs,
        out_shape=shapes,
        compiler_params=params(),
        cost_estimate=cost(20 * size, 28 * size, 2 * size),
        name=name,
    )(where, tabs, *sums, *args)


def permutations(groups, reps):
    flat = lambda f: [(g * reps + r, f(g, r)) for g in range(groups) for r in range(reps)]
    at = lambda g, r: g * reps + r
    far = []
    bit = 8
    while bit < reps:
        far.append(flat(lambda g, r, bit=bit: at(g, r ^ bit)))
        bit *= 2
    return {
        "core": flat(lambda g, r: at(g, r ^ 1)),
        "s1": flat(lambda g, r: at(g ^ (1 + r % 2), r)),
        "s2": flat(lambda g, r: at(g ^ (2 - r % 2), r)),
        "z1": flat(lambda g, r: at(g, r ^ (2 + 2 * (r % 2)))),
        "z2": flat(lambda g, r: at(g, r ^ (4 - 2 * (r % 2)))),
        "far": far,
    }


def local(groups, reps, hidden_in, out_grad, segment_ids, rand_blocks, w_qkv, w_out, w_in, w_down, vec_params, bias_hidden,
          moments_qkv, moments_out, moments_in, moments_down, moments_vec, moments_bias):
    perms = permutations(groups, reps)
    seqs, n, d = hidden_in.shape
    nb = rand_blocks.shape[1]
    g = lax.axis_index("group").astype(I32)
    r = lax.axis_index("rep").astype(I32)
    c, z = r % 2, (r // 2) % 4
    where = jnp.stack([g, c, z])
    one, two = 1 + c, 2 - c
    table = jnp.stack([2 * g + c, 2 * g + 1 - c, 2 * (g ^ one) + c, 2 * (g ^ one) + 1 - c,
                       2 * (g ^ two) + 1 - c, 2 * (g ^ two) + c, 2 * (g ^ 3) + c, 2 * (g ^ 3) + 1 - c])
    four = jnp.arange(4, dtype=I32)

    def turn(core, v):
        return jnp.where(core == 0, (v % 2) * 2 + v // 2, v)

    def order(core):
        return (turn(core, four ^ g)[:, None] * 4 + turn(core, four ^ z)[None, :]).reshape(16)

    tabs = jnp.concatenate([turn(c, four ^ z), turn(1 - c, four ^ z)])
    mine, other = order(c), order(1 - c)
    hm, ho = c[None], (1 - c)[None]

    pa = pack_a(where, w_qkv, vec_params.T, jnp.broadcast_to(bias_hidden[None], (8, bias_hidden.shape[0])))
    ga = gather(pa, perms)
    pb = pack_b(where, w_out, w_in, w_down)
    gb = gather(pb, perms)

    x = hidden_in.reshape(n, d)
    dy = out_grad.reshape(n, d)
    seg_col = jnp.broadcast_to(segment_ids.reshape(n, 1), (n, PAIR))
    rr = jnp.pad(rand_blocks[0].T, ((0, 0), (0, HEAD_DIM - nb)), constant_values=-1)
    rand_rows = jnp.concatenate([rr, rr], axis=1)

    qkv, wq_full, vec, bias = project(x, table, ga, groups)
    o, f = attn_fwd(qkv, seg_col, rand_rows, nb)
    y, dr1, hb, dh, x1b, dfb, dab, do, vs, bs = token(x, dy, o, vec, bias, table, gb)

    sums1 = reduce_all(grad_down(other, ho, hb, dfb, groups, 4), grad_down(mine, hm, hb, dfb, groups, 4), perms)
    sums2 = reduce_all(*[grad_cols(od, h, [(x1b, dh), (o, dab)], 16, None, "grad_in_out") for od, h in ((other, ho), (mine, hm))], perms)

    dq, dk, dv, qs = attn_bwd(qkv, f, o, do, seg_col, rand_rows, nb)
    vgrad = jnp.concatenate([qs[0:2], vs[2:8]], axis=0)
    small = jnp.concatenate([
        vgrad.reshape(4, 2, groups, d // groups).transpose(2, 0, 1, 3).reshape(groups, 4, 384),
        bs[:groups].reshape(groups, 2, 384),
        jnp.zeros((groups, 2, 384), F32),
    ], axis=1)
    small = small.reshape(groups, 2, 4, 384).transpose(0, 2, 1, 3).reshape(16, 2, 384)
    sums3 = reduce_all(*[grad_cols(od, h, [(x, dq), (x, dk), (x, dv)], 16, small, "grad_qkv") for od, h in ((other, ho), (mine, hm))], perms)
    gin = grad_input(dr1, dq, dk, dv, wq_full)

    count = 1.0 / (seqs * groups * reps)
    g_down, n_down, m_down = adam_down(where, tabs, sums1, w_down, moments_down, count)
    g_in, n_in, m_in, g_out, n_out, m_out = adam_cols(where, tabs, sums2, [(w_in, moments_in, 1, 4), (w_out, moments_out, 1, 1)], 0, count, "adam_in_out")
    g_qkv, n_qkv, m_qkv = adam_cols(where, tabs, sums3, [(w_qkv, moments_qkv, 3, 1)], 0, count, "adam_qkv")

    last = [jnp.concatenate([a[:, -1, :], b[:, -1, :]], axis=0) for a, b in ((sums3[0], sums3[1]), (sums3[2], sums3[3]))]
    own, sib = jnp.take(last[0], tabs[:4], axis=0), jnp.take(last[1], tabs[4:], axis=0)
    rows8 = jnp.where(c == 0, jnp.concatenate([own, sib]), jnp.concatenate([sib, own])).astype(F32) * count
    g_vec = rows8[:4].reshape(8, d // groups).T
    g_bias = rows8[4:6].reshape(-1)
    n_vec, m1, u1 = adam(vec_params, moments_vec[0], moments_vec[1], g_vec, 0.0)
    n_bias, m2, u2 = adam(bias_hidden, moments_bias[0], moments_bias[1], g_bias, 0.0)
    return (y.reshape(hidden_in.shape), gin.reshape(hidden_in.shape), g_qkv, g_out, g_in, g_down, g_vec, g_bias,
            n_qkv, n_out, n_in, n_down, n_vec, n_bias, m_qkv, m_out, m_in, m_down, jnp.stack([m1, u1]), jnp.stack([m2, u2]))


def solution(mesh):
    groups, reps = mesh.shape["group"], mesh.shape["rep"]
    tok = P(AX, None, None)
    row, mom = P("group", None), P(None, "group", None)

    def run(*args):
        return local(groups, reps, *args)

    return jax.shard_map(
        run,
        mesh=mesh,
        in_specs=(tok, tok, P(AX, None), tok, row, row, row, row, row, P("group"), mom, mom, mom, mom, mom, P(None, "group")),
        out_specs=(tok, tok, row, row, row, row, row, P("group"), row, row, row, row, row, P("group"), mom, mom, mom, mom, mom, P(None, "group")),
        check_vma=False,
    )
```

time: 970 us -> 408 us (0.42)
  waiting for transfers between devices: 428 us -> 114 us
  matrix products: 275 us -> 0 us
  Pallas kernels: 0 us -> 201 us
  other arithmetic: 116 us -> 30.9 us
  blocking collectives: 61.2 us -> 0 us
  local copies, waits for them, and re-layouts: 64.3 us -> 16.7 us
  starting transfers between devices: 0.41 us -> 36.8 us
  between operations: 15.7 us -> 1.68 us
    dot_general x18 -> x0, matrix products: 275 us -> none  [the longest x1 38.3 us: local(): jnp.dot(first_low, full_in, preferred_element_type=jnp.float32) + bias_full]
    reduce_scatter x3 -> x0, waiting for transfers between devices: 234 us -> none  [the longest x1 98.2 us: local(): lax.psum_scatter(grad_w_in, 'group', scatter_dimension=0, tiled=True)]
    pallas_call x0 -> x16, Pallas kernels: none -> 201 us  [the longest x1 38.9 us: token(): pl.pallas_call(kern, grid=(n // t,), in_specs=[SMEM, rows(w), rows(w), ro...]
    psum x1 -> x0, waiting for transfers between devices: 117 us -> none  [local(): lax.psum((shard_qkv, shard_out, shard_in, shard_down, shard_vec, shard_bi...]
    ppermute x0 -> x35, waiting for transfers between devices: none -> 114 us  [pperm(): return lax.ppermute(a, AX, pairs)]
    unnamed x136 -> x69, local copies, waits for them, and re-layouts: 50.2 us -> 5.48 us
    unnamed x12 -> x0, waiting for transfers between devices: 39.8 us -> none
    all_gather x4 -> x0, waiting for transfers between devices: 37.1 us -> none  [the longest x1 22.1 us: local(): lax.all_gather(w_qkv.astype(jnp.bfloat16), 'group', axis=0, tiled=True)]
  transfers between devices with their start and end apart: 10 -> 35, of which waited for: 7 -> 14; matrix products, arithmetic and copies ran while one was open for 22% -> 10% of each run, Pallas kernels for 0% -> 26%
where the time goes in v1:
time: 408 us; the launch traced here: 401 us
  Pallas kernels  201 us (49%)
  waiting for transfers between devices  114 us (28%)
  starting transfers between devices  36.8 us (9%)
  other arithmetic  30.9 us (8%)
  local copies, waits for them, and re-layouts  16.7 us (4%)
    ppermute x35, waiting for transfers between devices, pperm(): return lax.ppermute(a, AX, pairs)  114 us
    pallas_call x1, Pallas kernels, token(): pl.pallas_call(kern, grid=(n // t,), in_specs=[SMEM, rows(w), rows(w), ro...  38.9 us
    pallas_call x1, Pallas kernels, attn_bwd(): pl.pallas_call(lambda *refs: attn_bwd_kernel(nb, *refs), grid=(pairs,), i...  37.7 us
    ppermute x35, starting transfers between devices, pperm(): return lax.ppermute(a, AX, pairs)  36.8 us
    pallas_call x4, Pallas kernels, grad_cols(): pl.pallas_call(kern, grid_spec=pltpu.PrefetchScalarGridSpec(num_scalar_pr...  31.4 us
    pallas_call x1, Pallas kernels, attn_fwd(): pl.pallas_call(lambda *refs: attn_fwd_kernel(nb, *refs), grid=(pairs,), i...  27.2 us
    convert_element_type x15, other arithmetic, total(): return out.astype(BF)  23 us
    pallas_call x2, Pallas kernels, adam_cols(): pl.pallas_call(kern, grid=(4,), in_specs=[SMEM, SMEM] + [full(s.shape) fo...  16.2 us
  transfers between devices with their start and end apart: 35, of which 14 were waited for; matrix products, arithmetic and copies ran while one was open for 10% of the time, Pallas kernels for 26%

profile of v1, /device:TPU:0, one launch (start us, length us, event | category | flops | bytes accessed | tf_op | source)
XLA Modules:
  0.0 401.5 jit_solution(239668367929437801)
XLA Ops:
  8.6 30.2 %collective-permute-done.4.refs_1_ = bf16[2,9,96,768]{3,2,1,0:T(8,128)(2,1)S(1)} collective-permute-done((bf16[2,9,96,768]{3,2,1,0:T(8,128)(2,1)}, bf16[2,9,96,768]{3,2,1,0:T(8,128)(2,1)S(1)}, u32[]{:S(2)}, u32[]{:S(2)}) %collective-permute-start.4) | collective-permute-done | bytes 2654240 | tf_op jit(solution)/shard_map/ppermute | solution.py:263
  45.7 20.5 %collective-permute-done.refs_1_ = bf16[2,112,2304]{2,1,0:T(8,128)(2,1)} collective-permute-done((bf16[2,112,2304]{2,1,0:T(8,128)(2,1)}, bf16[2,112,2304]{2,1,0:T(8,128)(2,1)}, u32[]{:S(2)}, u32[]{:S(2)}) %collective-permute-start) | collective-permute-done | bytes 1032224 | tf_op jit(solution)/shard_map/ppermute | solution.py:263
  70.7 5.9 %collective-permute-done.2.refs_3_ = bf16[1,112,2304]{2,1,0:T(8,128)(2,1)} collective-permute-done((bf16[1,112,2304]{2,1,0:T(8,128)(2,1)S(1)}, bf16[1,112,2304]{2,1,0:T(8,128)(2,1)}, u32[]{:S(2)}, u32[]{:S(2)}) %collective-permute-start.2) | collective-permute-done | bytes 516128 | tf_op jit(solution)/shard_map/ppermute | solution.py:263
  79.8 9.1 %project.1 = (bf16[1024,2304]{1,0:T(8,128)(2,1)}, bf16[768,2304]{1,0:T(8,128)(2,1)}, f32[8,768]{1,0:T(8,128)}, f32[4,8,768]{2,1,0:T(8,128)}) custom-call(s32[8]{0:T(128)} %stack.61.tab_ref, bf16[1024,768]{1,0:T(8,128)(2,1)} %bitcast.64, bf16[2,112,2304]{2,1,0:T(8,128)(2,1)} %pack_a.1.refs_0_, bf16[2,112,2304]{2,1,0:T(8,128)(2,1)} %collective-permute-done.refs_1_, ...), custom_call_target="tpu_custom_call" | custom-call | flops 3623878656 | bytes 13369344 | tf_op jit(solution)/shard_map/project/pallas_call | solution.py:320
  90.0 27.2 %attn_fwd.1 = (bf16[1024,768]{1,0:T(8,128)(2,1)}, bf16[1024,768]{1,0:T(8,128)(2,1)}) custom-call(s32[1024,128]{1,0:T(8,128)} %broadcast_in_dim.34.refs_0_, s32[3,128]{1,0:T(4,128)} %pad_add_fusion.refs_1_, bf16[1024,2304]{1,0:T(8,128)(2,1)} %get-tuple-element.53.refs_2_.refs_3_.refs_4_, bf16[1024,2304]{1,0:T(8,128)(2,1)} %get-tuple-element.53.refs_2_.refs_3_.refs_4_, ...), custom_call_target="tpu_custom_call" | custom-call | tf_op jit(solution)/shard_map/attn_fwd/pallas_call | solution.py:112
  117.2 38.9 %token_.1 = (f32[1024,768]{1,0:T(8,128)}, f32[1024,768]{1,0:T(8,128)}, bf16[1024,3072]{1,0:T(8,128)(2,1)}, bf16[1024,3072]{1,0:T(8,128)(2,1)}, bf16[1024,768]{1,...) custom-call(s32[8]{0:T(128)} %stack.61.tab_ref, ...), custom_call_target="tpu_custom_call" | custom-call | flops 21743271936 | bytes 37355520 | tf_op jit(solution)/shard_map/token/pallas_call | solution.py:413
  156.1 37.7 %attn_bwd.1 = (bf16[1024,768]{1,0:T(8,128)(2,1)}, bf16[1024,768]{1,0:T(8,128)(2,1)}, bf16[1024,768]{1,0:T(8,128)(2,1)}, f32[8,768]{1,0:T(8,128)}) custom-call(s32[1024,128]{1,0:T(8,128)} %broadcast_in_dim.34.refs_0_, s32[3,128]{1,0:T(4,128)} %pad_add_fusion.refs_1_, bf16[1024,2304]{1,0:T(8,128)(2,1)} %get-tuple-element.53.refs_2_.refs_3_.refs_4_, ...), custom_call_target="tpu_custom_call" | custom-call | tf_op jit(solution)/shard_map/attn_bwd/pallas_call | solution.py:179
  195.6 6.7 %grad_qkv.3 = bf16[16,160,384]{2,1,0:T(8,128)(2,1)} custom-call(s32[16]{0:T(128)} %add.339.order_ref, s32[1]{0:T(128)} %bitcast.22.half_ref, bf16[1024,768]{1,0:T(8,128)(2,1)} %bitcast.66, bf16[1024,768]{1,0:T(8,128)(2,1)} %get-tuple-element.61.q_ref.refs_1_, bf16[1024,768]{1,0:T(8,128)(2,1)} %get-tuple-element.62.k_ref.refs_2_, ...), custom_call_target="tpu_custom_call" | custom-call | flops 1811939328 | bytes 5701632 | tf_op jit(solution)/shard_map/grad_qkv/pallas_call | solution.py:485
  202.3 8.8 %grad_in_out.3 = bf16[16,240,384]{2,1,0:T(8,128)(2,1)} custom-call(s32[16]{0:T(128)} %add.339.order_ref, s32[1]{0:T(128)} %bitcast.22.half_ref, bf16[1024,768]{1,0:T(8,128)(2,1)} %get-tuple-element.69.refs_0_, bf16[1024,768]{1,0:T(8,128)(2,1)} %get-tuple-element.54.o_ref.refs_6_.refs_1_, bf16[1024,3072]{1,0:T(8,128)(2,1)} %get-tuple-element.70.refs_2_, ...), custom_call_target="tpu_custom_call" | custom-call | flops 3019898880 | bytes 8454144 | tf_op jit(solution)/shard_map/grad_in_out/pallas_call | solution.py:485
  211.5 7.7 %grad_down.3 = bf16[16,96,768]{2,1,0:T(8,128)(2,1)} custom-call(s32[16]{0:T(128)} %add.339.order_ref, s32[1]{0:T(128)} %bitcast.22.half_ref, bf16[1024,3072]{1,0:T(8,128)(2,1)} %get-tuple-element.74.hb_ref, bf16[1024,768]{1,0:T(8,128)(2,1)} %get-tuple-element.75.dfb_ref), custom_call_target="tpu_custom_call" | custom-call | flops 2415919104 | bytes 7077888 | tf_op jit(solution)/shard_map/grad_down/pallas_call | solution.py:439
  220.5 6.7 %grad_qkv.2 = bf16[16,160,384]{2,1,0:T(8,128)(2,1)} custom-call(s32[16]{0:T(128)} %add.335.order_ref, s32[1]{0:T(128)} %bitcast.13.half_ref, bf16[1024,768]{1,0:T(8,128)(2,1)} %bitcast.67, bf16[1024,768]{1,0:T(8,128)(2,1)} %get-tuple-element.61.q_ref.refs_1_, bf16[1024,768]{1,0:T(8,128)(2,1)} %get-tuple-element.62.k_ref.refs_2_, ...), custom_call_target="tpu_custom_call" | custom-call | flops 1811939328 | bytes 5701632 | tf_op jit(solution)/shard_map/grad_qkv/pallas_call | solution.py:485
  232.0 7.4 %grad_down.2 = bf16[16,96,768]{2,1,0:T(8,128)(2,1)} custom-call(s32[16]{0:T(128)} %add.335.order_ref, s32[1]{0:T(128)} %bitcast.13.half_ref, bf16[1024,3072]{1,0:T(8,128)(2,1)} %get-tuple-element.74.hb_ref, bf16[1024,768]{1,0:T(8,128)(2,1)} %get-tuple-element.75.dfb_ref), custom_call_target="tpu_custom_call" | custom-call | flops 2415919104 | bytes 7077888 | tf_op jit(solution)/shard_map/grad_down/pallas_call | solution.py:439
  239.5 9.3 %grad_in_out.2 = bf16[16,240,384]{2,1,0:T(8,128)(2,1)} custom-call(s32[16]{0:T(128)} %add.335.order_ref, s32[1]{0:T(128)} %bitcast.13.half_ref, bf16[1024,768]{1,0:T(8,128)(2,1)} %get-tuple-element.69.refs_0_, bf16[1024,768]{1,0:T(8,128)(2,1)} %get-tuple-element.54.o_ref.refs_6_.refs_1_, bf16[1024,3072]{1,0:T(8,128)(2,1)} %get-tuple-element.70.refs_2_, ...), custom_call_target="tpu_custom_call" | custom-call | flops 3019898880 | bytes 8454144 | tf_op jit(solution)/shard_map/grad_in_out/pallas_call | solution.py:485
  257.0 5.0 %collective-permute-done.10 = bf16[4,160,384]{2,1,0:T(8,128)(2,1)S(1)} collective-permute-done((bf16[4,160,384]{2,1,0:T(8,128)(2,1)S(1)}, bf16[4,160,384]{2,1,0:T(8,128)(2,1)S(1)}, u32[]{:S(2)}, u32[]{:S(2)}) %collective-permute-start.10) | collective-permute-done | bytes 491552 | tf_op jit(solution)/shard_map/ppermute | solution.py:263
  265.3 5.9 %collective-permute-done.11 = bf16[2,160,384]{2,1,0:T(8,128)(2,1)S(1)} collective-permute-done((bf16[2,160,384]{2,1,0:T(8,128)(2,1)S(1)}, bf16[2,160,384]{2,1,0:T(8,128)(2,1)S(1)}, u32[]{:S(2)}, u32[]{:S(2)}) %collective-permute-start.11) | collective-permute-done | bytes 245792 | tf_op jit(solution)/shard_map/ppermute | solution.py:263
  285.3 4.4 %collective-permute-done.13 = bf16[1,160,384]{2,1,0:T(8,128)(2,1)S(1)} collective-permute-done((bf16[1,160,384]{2,1,0:T(8,128)(2,1)S(1)}, bf16[1,160,384]{2,1,0:T(8,128)(2,1)S(1)}, u32[]{:S(2)}, u32[]{:S(2)}) %collective-permute-start.13) | collective-permute-done | bytes 122912 | tf_op jit(solution)/shard_map/ppermute | solution.py:263
  295.9 8.9 %grad_input.1 = f32[1024,768]{1,0:T(8,128)} custom-call(f32[1024,768]{1,0:T(8,128)} %get-tuple-element.58.r_ref, bf16[1024,768]{1,0:T(8,128)(2,1)} %get-tuple-element.61.q_ref.refs_1_, bf16[1024,768]{1,0:T(8,128)(2,1)} %get-tuple-element.62.k_ref.refs_2_, bf16[1024,768]{1,0:T(8,128)(2,1)} %get-tuple-element.63.v_ref.refs_3_, ...), custom_call_target="tpu_custom_call" | custom-call | flops 3623878656 | bytes 14548992 | tf_op jit(solution)/shard_map/grad_input/pallas_call | solution.py:509
  322.4 7.7 %collective-permute-done.20 = bf16[2,240,384]{2,1,0:T(8,128)(2,1)} collective-permute-done((bf16[2,240,384]{2,1,0:T(8,128)(2,1)}, bf16[2,240,384]{2,1,0:T(8,128)(2,1)}, u32[]{:S(2)}, u32[]{:S(2)}) %collective-permute-start.20) | collective-permute-done | bytes 368672 | tf_op jit(solution)/shard_map/ppermute | solution.py:263
  332.4 7.6 %collective-permute-done.21 = bf16[1,240,384]{2,1,0:T(8,128)(2,1)S(1)} collective-permute-done((bf16[1,240,384]{2,1,0:T(8,128)(2,1)S(1)}, bf16[1,240,384]{2,1,0:T(8,128)(2,1)S(1)}, u32[]{:S(2)}, u32[]{:S(2)}) %collective-permute-start.21) | collective-permute-done | bytes 184352 | tf_op jit(solution)/shard_map/ppermute | solution.py:263
  345.6 13.0 %collective-permute-done.22 = bf16[1,240,384]{2,1,0:T(8,128)(2,1)S(1)} collective-permute-done((bf16[1,240,384]{2,1,0:T(8,128)(2,1)S(1)}, bf16[1,240,384]{2,1,0:T(8,128)(2,1)S(1)}, u32[]{:S(2)}, u32[]{:S(2)}) %collective-permute-start.22) | collective-permute-done | bytes 184352 | tf_op jit(solution)/shard_map/ppermute | solution.py:263
  362.1 7.2 %collective-permute-done.23.a1 = bf16[2,240,384]{2,1,0:T(8,128)(2,1)S(1)} collective-permute-done((bf16[2,240,384]{2,1,0:T(8,128)(2,1)S(1)}, bf16[2,240,384]{2,1,0:T(8,128)(2,1)S(1)}, u32[]{:S(2)}, u32[]{:S(2)}) %collective-permute-start.23) | collective-permute-done | bytes 368672 | tf_op jit(solution)/shard_map/ppermute | solution.py:263
  370.0 6.8 %adam_qkv.1 = (f32[192,2304]{1,0:T(8,128)}, f32[192,2304]{1,0:T(8,128)}, f32[2,192,2304]{2,1,0:T(8,128)}) custom-call(s32[3]{0:T(128)} %pad_add_fusion.1.where_ref, s32[8]{0:T(128)} %pad_add_fusion.2.tab_ref, bf16[2,160,384]{2,1,0:T(8,128)(2,1)} %copy-done.10, bf16[2,160,384]{2,1,0:T(8,128)(2,1)} %collective-permute-done.14.a1, ...), custom_call_target="tpu_custom_call" | custom-call | flops 8847360 | bytes 12386304 | tf_op jit(solution)/shard_map/adam_qkv/pallas_call | solution.py:622
  380.1 10.0 %adam_down.1 = (f32[768,768]{1,0:T(8,128)}, f32[768,768]{1,0:T(8,128)}, f32[2,768,768]{2,1,0:T(8,128)}) custom-call(s32[3]{0:T(128)} %pad_add_fusion.1.where_ref, s32[8]{0:T(128)} %pad_add_fusion.2.tab_ref, bf16[2,96,768]{2,1,0:T(8,128)(2,1)} %copy-done.6, bf16[2,96,768]{2,1,0:T(8,128)(2,1)} %copy-done.17, bf16[2,96,768]{2,1,0:T(8,128)(2,1)} %copy-done.18, ...), custom_call_target="tpu_custom_call" | custom-call | flops 11796480 | bytes 16515072 | tf_op jit(solution)/shard_map/adam_down/pallas_call | solution.py:575
  391.6 9.4 %adam_in_out.1 = (f32[192,3072]{1,0:T(8,128)}, f32[192,3072]{1,0:T(8,128)}, f32[2,192,3072]{2,1,0:T(8,128)}, f32[192,768]{1,0:T(8,128)}, f32[192,768]{1,0:T(8,128)}, /*index=5*/f32[2,192,768]{2,1,0:T(8,128)}) custom-call(s32[3]{0:T(128)} %pad_add_fusion.1.where_ref, s32[8]{0:T(128)} %pad_add_fusion.2.tab_ref, bf16[2,240,384]{2,1,0:T(8,128)(2,1)} %copy-done.5, ...), custom_call_target="tpu_custom_call" | custom-call | flops 14745600 | bytes 20643840 | tf_op jit(solution)/shard_map/adam_in_out/pallas_call | solution.py:622
  (201 shorter events, 97.8 us)
Async XLA Ops:
  5.7 33.1 %collective-permute-start.4 = (bf16[2,9,96,768]{3,2,1,0:T(8,128)(2,1)}, bf16[2,9,96,768]{3,2,1,0:T(8,128)(2,1)S(1)}, u32[]{:S(2)}, u32[]{:S(2)}) collective-permute-start(bf16[2,9,96,768]{3,2,1,0:T(8,128)(2,1)} %pack_b.1.refs_0_), channel_id=1, source_target_pairs={{0,8},{1,17},{2,10},{3,19},{4,12},{5,21},{6,14},{7,23},{8,0},{9,25... | collective-permute-start | bytes 7962632 | tf_op jit(solution)/shard_map/ppermute | solution.py:263
  38.9 31.7 %collective-permute-start.6 = (bf16[1,9,96,768]{3,2,1,0:T(8,128)(2,1)S(1)}, bf16[1,9,96,768]{3,2,1,0:T(8,128)(2,1)}, u32[]{:S(2)}, u32[]{:S(2)}) collective-permute-start(bf16[1,9,96,768]{3,2,1,0:T(8,128)(2,1)S(1)} %slice.329), channel_id=1, source_target_pairs={{0,16},{1,9},{2,18},{3,11},{4,20},{5,13},{6,22},{7,15},{8,24},{9,1... | collective-permute-start | bytes 3981320 | tf_op jit(solution)/shard_map/ppermute | solution.py:263
  41.0 76.2 %collective-permute-start.5 = (bf16[2,9,96,768]{3,2,1,0:T(8,128)(2,1)S(1)}, bf16[2,9,96,768]{3,2,1,0:T(8,128)(2,1)}, u32[]{:S(2)}, u32[]{:S(2)}) collective-permute-start(bf16[2,9,96,768]{3,2,1,0:T(8,128)(2,1)S(1)} %collective-permute-done.4.refs_1_), channel_id=1, source_target_pairs={{0,1},{1,0},{2,3},{3,2},{4,5},{5,4},{6,7},{7,6},{8,9},{9,8},{10,11... | collective-permute-start | bytes 7962632 | tf_op jit(solution)/shard_map/ppermute | solution.py:263
  44.2 22.0 %collective-permute-start = (bf16[2,112,2304]{2,1,0:T(8,128)(2,1)}, bf16[2,112,2304]{2,1,0:T(8,128)(2,1)}, u32[]{:S(2)}, u32[]{:S(2)}) collective-permute-start(bf16[2,112,2304]{2,1,0:T(8,128)(2,1)} %pack_a.1.refs_0_), channel_id=1, source_target_pairs={{0,8},{1,17},{2,10},{3,19},{4,12},{5,21},{6,14},{7,23},{8,0},{9,25... | collective-permute-start | bytes 3096584 | tf_op jit(solution)/shard_map/ppermute | solution.py:263
  69.1 10.7 %collective-permute-start.1 = (bf16[2,112,2304]{2,1,0:T(8,128)(2,1)}, bf16[2,112,2304]{2,1,0:T(8,128)(2,1)}, u32[]{:S(2)}, u32[]{:S(2)}) collective-permute-start(bf16[2,112,2304]{2,1,0:T(8,128)(2,1)} %collective-permute-done.refs_1_), channel_id=1, source_target_pairs={{0,1},{1,0},{2,3},{3,2},{4,5},{5,4},{6,7},{7,6},{8,9},{9,8},{10,11... | collective-permute-start | bytes 3096584 | tf_op jit(solution)/shard_map/ppermute | solution.py:263
  70.6 46.6 %collective-permute-start.7 = (bf16[1,9,96,768]{3,2,1,0:T(8,128)(2,1)}, bf16[1,9,96,768]{3,2,1,0:T(8,128)(2,1)}, u32[]{:S(2)}, u32[]{:S(2)}) collective-permute-start(bf16[1,9,96,768]{3,2,1,0:T(8,128)(2,1)} %collective-permute-done.6.refs_3_), channel_id=1, source_target_pairs={{0,1},{1,0},{2,3},{3,2},{4,5},{5,4},{6,7},{7,6},{8,9},{9,8},{10,11... | collective-permute-start | bytes 3981320 | tf_op jit(solution)/shard_map/ppermute | solution.py:263
  202.3 24.9 %collective-permute-start.8 = (bf16[16,160,384]{2,1,0:T(8,128)(2,1)}, bf16[16,160,384]{2,1,0:T(8,128)(2,1)S(1)}, u32[]{:S(2)}, u32[]{:S(2)}) collective-permute-start(bf16[16,160,384]{2,1,0:T(8,128)(2,1)} %grad_qkv.3), channel_id=1, source_target_pairs={{0,1},{1,0},{2,3},{3,2},{4,5},{5,4},{6,7},{7,6},{8,9},{9,8},{10,11... | collective-permute-start | bytes 5898248 | tf_op jit(solution)/shard_map/ppermute | solution.py:263
  211.0 42.8 %collective-permute-start.17 = (bf16[16,240,384]{2,1,0:T(8,128)(2,1)}, bf16[16,240,384]{2,1,0:T(8,128)(2,1)}, u32[]{:S(2)}, u32[]{:S(2)}) collective-permute-start(bf16[16,240,384]{2,1,0:T(8,128)(2,1)} %grad_in_out.3), channel_id=1, source_target_pairs={{0,1},{1,0},{2,3},{3,2},{4,5},{5,4},{6,7},{7,6},{8,9},{9,8},{10,11... | collective-permute-start | bytes 8847368 | tf_op jit(solution)/shard_map/ppermute | solution.py:263
  219.2 32.3 %collective-permute-start.26 = (bf16[16,96,768]{2,1,0:T(8,128)(2,1)}, bf16[16,96,768]{2,1,0:T(8,128)(2,1)}, u32[]{:S(2)}, u32[]{:S(2)}) collective-permute-start(bf16[16,96,768]{2,1,0:T(8,128)(2,1)} %grad_down.3), channel_id=1, source_target_pairs={{0,1},{1,0},{2,3},{3,2},{4,5},{5,4},{6,7},{7,6},{8,9},{9,8},{10,11... | collective-permute-start | bytes 7077896 | tf_op jit(solution)/shard_map/ppermute | solution.py:263
  230.3 18.5 %collective-permute-start.9 = (bf16[8,160,384]{2,1,0:T(8,128)(2,1)}, bf16[8,160,384]{2,1,0:T(8,128)(2,1)S(1)}, u32[]{:S(2)}, u32[]{:S(2)}) collective-permute-start(bf16[8,160,384]{2,1,0:T(8,128)(2,1)} %add_convert_fusion.2), channel_id=1, source_target_pairs={{0,8},{1,17},{2,10},{3,19},{4,12},{5,21},{6,14},{7,23},{8,0},{9,25... | collective-permute-start | bytes 2949128 | tf_op jit(solution)/shard_map/ppermute | solution.py:263
  249.9 12.1 %collective-permute-start.10 = (bf16[4,160,384]{2,1,0:T(8,128)(2,1)S(1)}, bf16[4,160,384]{2,1,0:T(8,128)(2,1)S(1)}, u32[]{:S(2)}, u32[]{:S(2)}) collective-permute-start(bf16[4,160,384]{2,1,0:T(8,128)(2,1)S(1)} %add_convert_fusion.5), channel_id=1, source_target_pairs={{0,16},{1,9},{2,18},{3,11},{4,20},{5,13},{6,22},{7,15},{8,24},{9,1... | collective-permute-start | bytes 1474568 | tf_op jit(solution)/shard_map/ppermute | solution.py:263
  253.1 28.9 %collective-permute-start.27 = (bf16[8,96,768]{2,1,0:T(8,128)(2,1)S(1)}, bf16[8,96,768]{2,1,0:T(8,128)(2,1)S(1)}, u32[]{:S(2)}, u32[]{:S(2)}) collective-permute-start(bf16[8,96,768]{2,1,0:T(8,128)(2,1)S(1)} %add_convert_fusion.1), channel_id=1, source_target_pairs={{0,8},{1,17},{2,10},{3,19},{4,12},{5,21},{6,14},{7,23},{8,0},{9,25... | collective-permute-start | bytes 3538952 | tf_op jit(solution)/shard_map/ppermute | solution.py:263
  255.6 36.6 %collective-permute-start.18 = (bf16[8,240,384]{2,1,0:T(8,128)(2,1)S(1)}, bf16[8,240,384]{2,1,0:T(8,128)(2,1)S(1)}, u32[]{:S(2)}, u32[]{:S(2)}) collective-permute-start(bf16[8,240,384]{2,1,0:T(8,128)(2,1)S(1)} %add_convert_fusion), channel_id=1, source_target_pairs={{0,8},{1,17},{2,10},{3,19},{4,12},{5,21},{6,14},{7,23},{8,0},{9,25... | collective-permute-start | bytes 4423688 | tf_op jit(solution)/shard_map/ppermute | solution.py:263
  279.1 10.6 %collective-permute-start.13 = (bf16[1,160,384]{2,1,0:T(8,128)(2,1)S(1)}, bf16[1,160,384]{2,1,0:T(8,128)(2,1)S(1)}, u32[]{:S(2)}, u32[]{:S(2)}) collective-permute-start(bf16[1,160,384]{2,1,0:T(8,128)(2,1)S(1)} %add_convert_fusion.13), channel_id=1, source_target_pairs={{0,4},{1,3},{2,6},{3,1},{4,0},{5,7},{6,2},{7,5},{8,12},{9,11},{10,... | collective-permute-start | bytes 368648 | tf_op jit(solution)/shard_map/ppermute | solution.py:263
  283.7 21.7 %collective-permute-start.28 = (bf16[4,96,768]{2,1,0:T(8,128)(2,1)S(1)}, bf16[4,96,768]{2,1,0:T(8,128)(2,1)S(1)}, u32[]{:S(2)}, u32[]{:S(2)}) collective-permute-start(bf16[4,96,768]{2,1,0:T(8,128)(2,1)S(1)} %add_convert_fusion.4), channel_id=1, source_target_pairs={{0,16},{1,9},{2,18},{3,11},{4,20},{5,13},{6,22},{7,15},{8,24},{9,1... | collective-permute-start | bytes 1769480 | tf_op jit(solution)/shard_map/ppermute | solution.py:263
  289.7 15.1 %collective-permute-start.14 = (bf16[2,160,384]{2,1,0:T(8,128)(2,1)S(1)}, bf16[2,160,384]{2,1,0:T(8,128)(2,1)}, u32[]{:S(2)}, u32[]{:S(2)}) collective-permute-start(bf16[2,160,384]{2,1,0:T(8,128)(2,1)S(1)} %pad_maximum_fusion.2.a0), channel_id=1, source_target_pairs={{0,2},{1,5},{2,0},{3,7},{4,6},{5,1},{6,4},{7,3},{8,10},{9,13},{10,... | collective-permute-start | bytes 737288 | tf_op jit(solution)/shard_map/ppermute | solution.py:263
  295.6 17.4 %collective-permute-start.19 = (bf16[4,240,384]{2,1,0:T(8,128)(2,1)}, bf16[4,240,384]{2,1,0:T(8,128)(2,1)}, u32[]{:S(2)}, u32[]{:S(2)}) collective-permute-start(bf16[4,240,384]{2,1,0:T(8,128)(2,1)} %add_convert_fusion.3), channel_id=1, source_target_pairs={{0,16},{1,9},{2,18},{3,11},{4,20},{5,13},{6,22},{7,15},{8,24},{9,1... | collective-permute-start | bytes 2211848 | tf_op jit(solution)/shard_map/ppermute | solution.py:263
  315.1 14.9 %collective-permute-start.20 = (bf16[2,240,384]{2,1,0:T(8,128)(2,1)}, bf16[2,240,384]{2,1,0:T(8,128)(2,1)}, u32[]{:S(2)}, u32[]{:S(2)}) collective-permute-start(bf16[2,240,384]{2,1,0:T(8,128)(2,1)} %add_convert_fusion.6), channel_id=1, source_target_pairs={{0,2},{1,5},{2,0},{3,7},{4,6},{5,1},{6,4},{7,3},{8,10},{9,13},{10,... | collective-permute-start | bytes 1105928 | tf_op jit(solution)/shard_map/ppermute | solution.py:263
  319.4 22.0 %collective-permute-start.30 = (bf16[1,96,768]{2,1,0:T(8,128)(2,1)S(1)}, bf16[1,96,768]{2,1,0:T(8,128)(2,1)S(1)}, u32[]{:S(2)}, u32[]{:S(2)}) collective-permute-start(bf16[1,96,768]{2,1,0:T(8,128)(2,1)S(1)} %add_convert_fusion.12), channel_id=1, source_target_pairs={{0,4},{1,3},{2,6},{3,1},{4,0},{5,7},{6,2},{7,5},{8,12},{9,11},{10,... | collective-permute-start | bytes 442376 | tf_op jit(solution)/shard_map/ppermute | solution.py:263
  341.3 17.4 %collective-permute-start.22 = (bf16[1,240,384]{2,1,0:T(8,128)(2,1)S(1)}, bf16[1,240,384]{2,1,0:T(8,128)(2,1)S(1)}, u32[]{:S(2)}, u32[]{:S(2)}) collective-permute-start(bf16[1,240,384]{2,1,0:T(8,128)(2,1)S(1)} %add_convert_fusion.9), channel_id=1, source_target_pairs={{0,4},{1,3},{2,6},{3,1},{4,0},{5,7},{6,2},{7,5},{8,12},{9,11},{10,... | collective-permute-start | bytes 552968 | tf_op jit(solution)/shard_map/ppermute | solution.py:263
  342.7 19.2 %collective-permute-start.31 = (bf16[1,96,768]{2,1,0:T(8,128)(2,1)S(1)}, bf16[1,96,768]{2,1,0:T(8,128)(2,1)S(1)}, u32[]{:S(2)}, u32[]{:S(2)}) collective-permute-start(bf16[1,96,768]{2,1,0:T(8,128)(2,1)S(1)} %add_convert_fusion.11), channel_id=1, source_target_pairs={{0,4},{1,3},{2,6},{3,1},{4,0},{5,7},{6,2},{7,5},{8,12},{9,11},{10,... | collective-permute-start | bytes 442376 | tf_op jit(solution)/shard_map/ppermute | solution.py:263
  361.9 15.4 %collective-permute-start.32 = (bf16[2,96,768]{2,1,0:T(8,128)(2,1)S(1)}, bf16[2,96,768]{2,1,0:T(8,128)(2,1)S(1)}, u32[]{:S(2)}, u32[]{:S(2)}) collective-permute-start(bf16[2,96,768]{2,1,0:T(8,128)(2,1)S(1)} %pad_maximum_fusion.1.a0), channel_id=1, source_target_pairs={{0,2},{1,5},{2,0},{3,7},{4,6},{5,1},{6,4},{7,3},{8,10},{9,13},{10,... | collective-permute-start | bytes 884744 | tf_op jit(solution)/shard_map/ppermute | solution.py:263
  362.0 28.1 %collective-permute-start.24 = (bf16[2,240,384]{2,1,0:T(8,128)(2,1)S(1)}, bf16[2,240,384]{2,1,0:T(8,128)(2,1)S(1)}, u32[]{:S(2)}, u32[]{:S(2)}) collective-permute-start(bf16[2,240,384]{2,1,0:T(8,128)(2,1)S(1)} %pad_maximum_fusion.a0), channel_id=1, source_target_pairs={{0,1},{1,0},{2,3},{3,2},{4,5},{5,4},{6,7},{7,6},{8,9},{9,8},{10,11... | collective-permute-start | bytes 1105928 | tf_op jit(solution)/shard_map/ppermute | solution.py:263
  369.3 20.8 %collective-permute-start.25 = (bf16[2,240,384]{2,1,0:T(8,128)(2,1)S(1)}, bf16[2,240,384]{2,1,0:T(8,128)(2,1)S(1)}, u32[]{:S(2)}, u32[]{:S(2)}) collective-permute-start(bf16[2,240,384]{2,1,0:T(8,128)(2,1)S(1)} %collective-permute-done.23.a1), channel_id=1, source_target_pairs={{0,1},{1,0},{2,3},{3,2},{4,5},{5,4},{6,7},{7,6},{8,9},{9,8},{10,11... | collective-permute-start | bytes 1105928 | tf_op jit(solution)/shard_map/ppermute | solution.py:263
  (42 other events, 455.3 us)
